TPU v7x, 32 devices: a whole 2x2x4 slice. The times are simulated.
32 devices in a mesh: grp: 2 (over y), seq: 4 (over z), head: 2 (over x), tp: 2 (over core).
Axes of the slice: x: 2, y: 2, z: 4, core: 2. Of those that a mesh axis runs over, the one named last changes fastest.
Arguments:
- queries: bfloat16 [16384, 16, 128], P(('grp', 'seq'), ('head', 'tp')), parts along dimension 0, may hold values from -6 to 6
- key_rows: bfloat16 [16384, 16, 128], P(('grp', 'seq'), ('head', 'tp')), parts along dimension 0, may hold values from -6 to 6
- values: bfloat16 [16384, 16, 128], P(('grp', 'seq'), ('head', 'tp')), parts along dimension 0, may hold values from -6 to 6
- log_decay: float32 [16, 16384], P(('head', 'tp'), ('grp', 'seq')), parts along dimension 1, may hold values from -1 to 0
- write_rate: float32 [16, 16384], P(('head', 'tp'), ('grp', 'seq')), parts along dimension 1, may hold values from 0.002 to 0.05
- router_weight: bfloat16 [16, 128, 256], P(('head', 'tp')), may hold values from -100 to 100
- teacher_logits: bfloat16 [8, 4, 4, 128, 256], P(('grp', 'seq'), ('head', 'tp')), parts along dimension 0, may hold values from -400 to 400
- span_length: int32 [8, 4, 128], P(('grp', 'seq'), ('head', 'tp')), parts along dimension 0, may hold values from 1 to 16, 512 in all within a row
- span_owner: int32 [8, 4, 128, 1], P(('grp', 'seq'), ('head', 'tp')), parts along dimension 0, may hold values from 0 to 3; in each aligned block of 128 rows (0 to 127, 128 to 255, ..., all dimensions but the last counted through in order) at most 128 rows name the same one
Outputs:
- grad_router: float32 [32, 128, 256], P(('grp', 'head', 'tp')), parts along dimension 0
- grad_heads: float32 [16384, 16, 128], P(('grp', 'seq'), ('head', 'tp')), parts along dimension 0
- mean_kl: float32 [2], P('grp'), parts along dimension 0
There are 2 independent parts, one for each index of `grp`. A program takes and returns all parts, laid end to end along the dimension named above; an argument that names none is the same for every part. Nothing has to cross between parts.
Inputs may be any that keep to these rules, and one draw needn't show every extreme that they name: `span_length`: the lengths of one region sum to 512. `span_owner`: among the tokens of one region no owner is named more than 128 times; some owner is named exactly 128 times in some regions.
All inputs are finite; a program needn't handle non-finite values.
Results may differ from a plain program's by a relative error of at most 0.008.
Values may be sent and summed in bfloat16 or wider, within the bound.
A program may use at most 128 MiB of HBM per device.

v0:
```python
import jax
import jax.numpy as jnp
from jax import lax
from jax.sharding import PartitionSpec as P

BLOCK = 128


UPPER_LIMIT = lax.Precision.HIGHEST


def shifted(value, axis, steps):
    count = lax.axis_size(axis)
    leading, last = (max(0, -steps), min(count, count - steps))
    return lax.ppermute(value, axis, [(source, source + steps) for source in range(leading, last)])


def unit_rows(array):
    return array / jnp.sqrt(jnp.sum(array * array, axis=-1, keepdims=True) + 1e-06)


def log_probs(logits):
    top = jnp.max(logits, axis=-1, keepdims=True)
    displaced_sums = logits - top
    return displaced_sums - jnp.log(jnp.sum(jnp.exp(displaced_sums), axis=-1, keepdims=True))


def apply_map(first, second):
    return jnp.einsum("hij,hjk->hik", first, second, precision=UPPER_LIMIT)


def combine_maps(earlier, later):
    return (apply_map(later[0], earlier[0]), apply_map(later[0], earlier[1]) + later[1])


def member_rows(length_lists, region):
    starts = jnp.cumsum(length_lists, axis=-1) - length_lists
    positions = lax.broadcasted_iota(jnp.int32, length_lists.shape + (region,), 2)
    inside = (positions >= starts[..., None]) & (positions < (starts + length_lists)[..., None])
    return inside.astype(jnp.float32)


def unit_lower_inverse(strict_part, size):
    negated = -strict_part
    inverse = jnp.eye(size, dtype=jnp.float32) + negated
    power = negated
    for level in range((size - 1).bit_length() - 1):
        power = apply_map(power, power)
        inverse = inverse + apply_map(inverse, power)
    return inverse


def block_terms(query_low, keyed_low, value, decay, rate):
    size = query_low.shape[1]
    width = query_low.shape[2]
    keyed = keyed_low.astype(jnp.float32)
    query = query_low.astype(jnp.float32)
    cumul = jnp.cumsum(decay, axis=-1)
    row_ids = lax.broadcasted_iota(jnp.int32, (size, size), 0)
    col_ids = lax.broadcasted_iota(jnp.int32, (size, size), 1)
    closed_prefix_sums = row_ids >= col_ids
    strict = row_ids > col_ids
    ratio = jnp.exp(jnp.where(closed_prefix_sums, cumul[:, :, None] - cumul[:, None, :], -1e30))
    gamma = jnp.exp(cumul)
    key_key = jnp.einsum("ntd,nsd->nts", keyed_low, keyed_low, preferred_element_type=jnp.float32)
    strict_part = rate[:, :, None] * jnp.where(strict, ratio * key_key, 0.0)
    right = rate[:, :, None] * jnp.concatenate([value, gamma[:, :, None] * keyed], axis=-1)
    inverse = unit_lower_inverse(strict_part, size)
    solved = jnp.einsum("nts,nsd->ntd", inverse, right, precision=UPPER_LIMIT)
    write_portion = solved[:, :, :width]
    erase_part = solved[:, :, width:]
    query_key = jnp.einsum("ntd,nsd->nts", query_low, keyed_low, preferred_element_type=jnp.float32)
    mixer = jnp.where(closed_prefix_sums, ratio * query_key, 0.0)
    local_out = jnp.einsum("nts,nsd->ntd", mixer, write_portion, precision=UPPER_LIMIT)
    reach = gamma[:, :, None] * query - jnp.einsum(
        "nts,nsd->ntd", mixer, erase_part, precision=UPPER_LIMIT
    )
    trailing_keys = keyed * ratio[:, -1, :, None]
    block_map = gamma[:, -1, None, None] * jnp.eye(width, dtype=jnp.float32) - jnp.einsum(
        "nsk,nsj->nkj", trailing_keys, erase_part, precision=UPPER_LIMIT
    )
    block_increment = jnp.einsum(
        "qoa,qoi->qai", trailing_keys, write_portion, precision=UPPER_LIMIT
    )
    return (local_out, reach, block_map, block_increment)


def shards(
    queries,
    key_rows,
    values,
    log_decay,
    write_rate,
    router_weight,
    teacher_logits,
    span_length,
    span_owner,
):
    rows, heads, width = queries.shape
    blocks = rows // BLOCK

    def arrange(array):
        return jnp.transpose(array, (1, 0, 2)).reshape(heads * blocks, BLOCK, width)

    query = arrange(unit_rows(queries.astype(jnp.float32)).astype(jnp.bfloat16))
    keyed = arrange(unit_rows(key_rows.astype(jnp.float32)).astype(jnp.bfloat16))
    value = arrange(values.astype(jnp.float32))
    decay = log_decay.reshape(heads * blocks, BLOCK)
    rate = write_rate.reshape(heads * blocks, BLOCK)
    terms = block_terms(query, keyed, value, decay, rate)

    def by_block(array):
        return jnp.swapaxes(array.reshape((heads, blocks) + array.shape[1:]), 0, 1)

    local_out, reach, block_map, block_increment = [by_block(item) for item in terms]
    identity = jnp.broadcast_to(jnp.eye(width, dtype=jnp.float32), (heads, width, width))
    empty = jnp.zeros((heads, width, width), jnp.float32)

    def compose(carry, pair):
        return (combine_maps(carry, pair), None)

    (dev_map, dev_add), _ = lax.scan(compose, (identity, empty), (block_map, block_increment))

    def relay(step, incoming):
        outgoing = apply_map(dev_map, incoming) + dev_add
        return shifted(outgoing, "seq", 1)

    state_in = lax.fori_loop(0, lax.axis_size("seq") - 1, relay, empty)

    def emit(recurrent_state, pieces):
        block_extent, block_within, one_map, one_add = pieces
        output_rows = (
            jnp.einsum("aci,aie->ace", block_extent, recurrent_state, precision=UPPER_LIMIT)
            + block_within
        )
        return (apply_map(one_map, recurrent_state) + one_add, output_rows)

    _, head_out = lax.scan(emit, state_in, (reach, local_out, block_map, block_increment))
    head_out = jnp.transpose(head_out, (0, 2, 1, 3)).reshape(rows, heads, width)
    scale = jnp.sqrt(jnp.mean(head_out * head_out, axis=-1, keepdims=True) + 1e-06)
    unit = head_out / scale
    normed = unit.astype(jnp.bfloat16)
    region = rows // lax.axis_size(("head", "tp"))
    lengths = span_length.reshape(-1)
    owners = span_owner.reshape(-1)
    count_tok = lengths.shape[0]
    batch_sample_number = lax.axis_size("seq")
    capacity = teacher_logits.shape[3]
    experts = teacher_logits.shape[4]
    span_len = lengths.astype(jnp.float32)[:, None]
    member = member_rows(lengths.reshape(1, count_tok), region)[0]
    piece = normed
    region_logits = lax.psum_scatter(
        jnp.einsum("rhd,hde->re", piece, router_weight, preferred_element_type=jnp.float32),
        ("head", "tp"),
        scatter_dimension=0,
        tiled=True,
    )
    averaged_groups = jnp.dot(member, region_logits, precision=UPPER_LIMIT) / span_len
    token_row = lax.broadcasted_iota(jnp.int32, (count_tok, count_tok), 0)
    token_col = lax.broadcasted_iota(jnp.int32, (count_tok, count_tok), 1)
    same = owners[:, None] == owners[None, :]
    slots = jnp.sum((same & (token_col < token_row)).astype(jnp.int32), axis=1)
    target = owners * capacity + slots
    placing = (
        target[:, None]
        == lax.broadcasted_iota(jnp.int32, (count_tok, batch_sample_number * capacity), 1)
    ).astype(jnp.float32)
    outgoing = jnp.dot(placing.T, averaged_groups, precision=UPPER_LIMIT).reshape(
        batch_sample_number, capacity, experts
    )
    owner_ids = lax.broadcasted_iota(jnp.int32, (batch_sample_number, count_tok), 0)
    counts = jnp.sum((owners[None, :] == owner_ids).astype(jnp.int32), axis=1, keepdims=True)
    arrived, arrived_counts = (
        lax.all_to_all(outgoing, "seq", split_axis=0, concat_axis=0, tiled=True),
        lax.all_to_all(counts, "seq", split_axis=0, concat_axis=0, tiled=True),
    )
    teacher_lp = log_probs(
        teacher_logits.reshape(batch_sample_number, capacity, experts).astype(jnp.float32)
    )
    student_lp = log_probs(arrived)
    teacher_p = jnp.exp(teacher_lp)
    valid = (
        lax.broadcasted_iota(jnp.int32, (batch_sample_number, capacity), 1) < arrived_counts
    ).astype(jnp.float32)
    kl_part = jnp.sum(valid * jnp.sum(teacher_p * (teacher_lp - student_lp), axis=-1))
    slot_grad = (jnp.exp(student_lp) - teacher_p) * valid[:, :, None]
    returned = lax.all_to_all(slot_grad, "seq", split_axis=0, concat_axis=0, tiled=True)
    token_grad = jnp.dot(
        placing, returned.reshape(batch_sample_number * capacity, experts), precision=UPPER_LIMIT
    )
    scaled_grad = token_grad / span_len
    row_grad = jnp.dot(member.T, scaled_grad, precision=UPPER_LIMIT).astype(jnp.bfloat16)
    piece = lax.all_gather(row_grad, ("head", "tp"), axis=0, tiled=True)
    weight_grad = jnp.einsum("rhd,re->hde", normed, piece, preferred_element_type=jnp.float32)
    update = jnp.einsum("re,hde->rhd", piece, router_weight, preferred_element_type=jnp.float32)
    state_grad = update
    weight_grad, state_grad = (weight_grad, state_grad)
    grad_router = lax.psum(weight_grad, "seq")
    grad_heads = (state_grad - unit * jnp.mean(state_grad * unit, axis=-1, keepdims=True)) / scale
    tokens_all = count_tok * batch_sample_number * lax.axis_size(("head", "tp"))
    mean_kl = (lax.psum(kl_part, ("seq", "head", "tp")) / tokens_all).reshape(1)
    return (grad_router, grad_heads, mean_kl)


def solution(mesh):
    placed = (
        P(("grp", "seq"), ("head", "tp"), None),
        P(("grp", "seq"), ("head", "tp"), None),
        P(("grp", "seq"), ("head", "tp"), None),
        P(("head", "tp"), ("grp", "seq")),
        P(("head", "tp"), ("grp", "seq")),
        P(("head", "tp"), None, None),
        P(("grp", "seq"), ("head", "tp"), None, None, None),
        P(("grp", "seq"), ("head", "tp"), None),
        P(("grp", "seq"), ("head", "tp"), None, None),
    )
    return jax.shard_map(
        shards,
        mesh=mesh,
        in_specs=placed,
        out_specs=(
            P(("grp", "head", "tp"), None, None),
            P(("grp", "seq"), ("head", "tp"), None),
            P("grp"),
        ),
        check_vma=False,
    )
```

profile of v0, /device:TPU:0, one launch (start us, length us, event | category | flops | bytes accessed | tf_op | source)
XLA Modules:
  0.0 492.5 jit_solution(11891066219587129904)
XLA Ops:
  7.3 4.8 fusion.27
  12.4 4.9 %fusion.47 = bf16[4,2048,128]{2,0,1:T(4,128)(2,1)S(1)} fusion(bf16[2048,4,128]{2,1,0:T(4,128)(2,1)S(1)} %copy-done.4, f32[2048,4]{1,0:T(8,128)S(1)} %add_sqrt_fusion.1), kind=kLoop, calls=%fused_computation.73 | loop fusion | flops 3145728 | bytes 4227072 | tf_op jit(solution)/shard_map/transpose | solution.py:103
  17.7 3.6 fusion.118
  21.6 10.7 %fusion.45 = f32[64,128,128]{2,1,0:T(8,128)S(1)} fusion(f32[64,128,128]{2,1,0:T(8,128)} %fusion.118, f32[64,128]{1,0:T(8,128)S(1)} %mul.118, f32[64,128]{1,0:T(8,128)S(1)} %reduce_window_sum.18, pred[128,128]{1,0:T(8,128)(4,1)S(1)} %get-tuple-element.163, pred[128,128]{1,0:T(8,128)(4,1)S(1)} %get-tuple-element.164), kind=kOutput, calls=%fused_computation.71 | convolution fusion | flops 1616904192 | bytes 8486912 | tf_op jit(solution)/shard_map/hij,hjk->hik/dot_general | solution.py:29
  32.4 5.1 %fusion.119 = f32[64,128,128]{2,1,0:T(8,128)S(1)} fusion(f32[64,128,128]{2,1,0:T(8,128)S(1)} %fusion.45), kind=kOutput, calls=%fused_computation.166 | convolution fusion | flops 1610612736 | bytes 8388608 | tf_op jit(solution)/shard_map/hij,hjk->hik/dot_general | solution.py:29
  37.4 8.7 %add_add_fusion = f32[64,128,128]{2,1,0:T(8,128)S(1)} fusion(f32[64,128,128]{2,1,0:T(8,128)S(1)} %fusion.45, f32[64,128,128]{2,1,0:T(8,128)S(1)} %copy-done.6, f32[64,128]{1,0:T(8,128)S(1)} %mul.118, f32[64,128]{1,0:T(8,128)S(1)} %reduce_window_sum.18, f32[128,128]{1,0:T(8,128)S(1)} %fusion.106, pred[128,128]{1,0:T(8,128)(4,1)S(1)} %get-tuple-element.163, ...), kind=kOutput, calls=%fused_computation.63 | convolution fusion | flops 1626341376 | bytes 12746752 | tf_op jit(solution)/shard_map/hij,hjk->hik/dot_general | solution.py:29
  46.2 5.1 %fusion.121 = f32[64,128,128]{2,1,0:T(8,128)S(1)} fusion(f32[64,128,128]{2,1,0:T(8,128)S(1)} %fusion.119), kind=kOutput, calls=%fused_computation.168 | convolution fusion | flops 1610612736 | bytes 8388608 | tf_op jit(solution)/shard_map/hij,hjk->hik/dot_general | solution.py:29
  51.2 6.0 %fusion.120 = f32[64,128,128]{2,1,0:T(8,128)} fusion(f32[64,128,128]{2,1,0:T(8,128)S(1)} %add_add_fusion, f32[64,128,128]{2,1,0:T(8,128)S(1)} %fusion.119), kind=kOutput, calls=%fused_computation.167 | convolution fusion | flops 1610612736 | bytes 12582912 | tf_op jit(solution)/shard_map/hij,hjk->hik/dot_general | solution.py:29
  57.3 5.1 %fusion.122 = f32[64,128,128]{2,1,0:T(8,128)S(1)} fusion(f32[64,128,128]{2,1,0:T(8,128)S(1)} %fusion.121), kind=kOutput, calls=%fused_computation.169 | convolution fusion | flops 1610612736 | bytes 8388608 | tf_op jit(solution)/shard_map/hij,hjk->hik/dot_general | solution.py:29
  62.4 8.0 %convolution_add_fusion.5 = f32[64,128,128]{2,1,0:T(8,128)S(1)} fusion(f32[64,128,128]{2,1,0:T(8,128)S(1)} %fusion.121, f32[64,128,128]{2,1,0:T(8,128)S(1)} %add_add_fusion, f32[64,128,128]{2,1,0:T(8,128)} %fusion.120), kind=kOutput, calls=%fused_computation.69 | convolution fusion | flops 1612709888 | bytes 16777216 | tf_op jit(solution)/shard_map/hij,hjk->hik/dot_general | solution.py:29
  70.4 5.6 %fusion.124 = f32[64,128,128]{2,1,0:T(8,128)S(1)} fusion(f32[64,128,128]{2,1,0:T(8,128)S(1)} %fusion.122), kind=kOutput, calls=%fused_computation.171 | convolution fusion | flops 1610612736 | bytes 8388608 | tf_op jit(solution)/shard_map/hij,hjk->hik/dot_general | solution.py:29
  76.0 5.8 %fusion.123 = f32[64,128,128]{2,1,0:T(8,128)} fusion(f32[64,128,128]{2,1,0:T(8,128)S(1)} %convolution_add_fusion.5, f32[64,128,128]{2,1,0:T(8,128)S(1)} %fusion.122), kind=kOutput, calls=%fused_computation.170 | convolution fusion | flops 1610612736 | bytes 12582912 | tf_op jit(solution)/shard_map/hij,hjk->hik/dot_general | solution.py:29
  81.8 5.1 %fusion.125 = f32[64,128,128]{2,1,0:T(8,128)S(1)} fusion(f32[64,128,128]{2,1,0:T(8,128)S(1)} %fusion.124), kind=kOutput, calls=%fused_computation.172 | convolution fusion | flops 1610612736 | bytes 8388608 | tf_op jit(solution)/shard_map/hij,hjk->hik/dot_general | solution.py:29
  86.9 8.0 %convolution_add_fusion.4 = f32[64,128,128]{2,1,0:T(8,128)S(1)} fusion(f32[64,128,128]{2,1,0:T(8,128)S(1)} %fusion.124, f32[64,128,128]{2,1,0:T(8,128)S(1)} %convolution_add_fusion.5, f32[64,128,128]{2,1,0:T(8,128)} %fusion.123), kind=kOutput, calls=%fused_computation.67 | convolution fusion | flops 1612709888 | bytes 16777216 | tf_op jit(solution)/shard_map/hij,hjk->hik/dot_general | solution.py:29
  94.9 3.1 convert_multiply_fusion.1
  98.5 2.2 copy.65
  101.0 3.7 fusion.29
  104.9 4.9 %fusion.46 = bf16[4,2048,128]{2,0,1:T(4,128)(2,1)S(1)} fusion(bf16[2048,4,128]{2,1,0:T(4,128)(2,1)S(1)} %copy-done.5, f32[2048,4]{1,0:T(8,128)S(1)} %add_sqrt_fusion), kind=kLoop, calls=%fused_computation.72 | loop fusion | flops 3145728 | bytes 4227072 | tf_op jit(solution)/shard_map/transpose | solution.py:103
  111.7 5.8 %fusion.126 = f32[64,128,128]{2,1,0:T(8,128)} fusion(f32[64,128,128]{2,1,0:T(8,128)S(1)} %convolution_add_fusion.4, f32[64,128,128]{2,1,0:T(8,128)S(1)} %fusion.125), kind=kOutput, calls=%fused_computation.173 | convolution fusion | flops 1610612736 | bytes 12582912 | tf_op jit(solution)/shard_map/hij,hjk->hik/dot_general | solution.py:29
  117.6 12.2 %fusion.22 = f32[64,128,256]{2,1,0:T(8,128)S(1)} fusion(f32[64,128,128]{2,1,0:T(8,128)} %convert_multiply_fusion.1, f32[64,128,128]{2,1,0:T(8,128)} %bitcast.158, f32[64,128]{1,0:T(8,128)S(1)} %mul.118, f32[64,128,128]{2,1,0:T(8,128)S(1)} %convolution_add_fusion.4, f32[64,128,128]{2,1,0:T(8,128)} %fusion.126), kind=kOutput, calls=%fused_computation.27 | convolution fusion | flops 3226468352 | bytes 25198592 | tf_op jit(solution)/shard_map/nts,nsd->ntd/dot_general | solution.py:69
  129.8 8.2 %multiply_subtract_fusion = f32[64,128,128]{2,1,0:T(8,128)} fusion(bf16[64,128,128]{2,1,0:T(8,128)(2,1)S(1)} %bitcast.152, f32[64,128]{1,0:T(8,128)S(1)} %exp.22, f32[64,128,256]{2,1,0:T(8,128)S(1)} %fusion.22, f32[64,128,128]{2,1,0:T(8,128)S(1)} %fusion.127, f32[64,128]{1,0:T(8,128)S(1)} %reduce_window_sum.18, pred[128,128]{1,0:T(8,128)(4,1)S(1)} %get-tuple-element.164), kind=kOutput, calls=%fused_computation.51 | convolution fusion | flops 1617952768 | bytes 14794752 | tf_op jit(solution)/shard_map/nts,nsd->ntd/dot_general | solution.py:75
  138.0 6.7 %fusion.33 = f32[64,128,128]{2,1,0:T(8,128)} fusion(f32[64,128,256]{2,1,0:T(8,128)S(1)} %fusion.22, f32[64,128,128]{2,1,0:T(8,128)S(1)} %fusion.127, f32[64,128]{1,0:T(8,128)S(1)} %reduce_window_sum.18, pred[128,128]{1,0:T(8,128)(4,1)S(1)} %get-tuple-element.164), kind=kOutput, calls=%fused_computation.57 | convolution fusion | flops 1614807040 | bytes 12664832 | tf_op jit(solution)/shard_map/nts,nsd->ntd/dot_general | solution.py:74
  144.6 3.5 select_exponential_fusion
  148.3 5.0 %copy.86 = f32[4,16,128,128]{3,2,0,1:T(8,128)} copy(f32[4,16,128,128]{3,2,1,0:T(8,128)} %bitcast.153) | data formatting | bytes 8388608 | tf_op jit(solution)/shard_map/reshape | solution.py:113
  153.3 2.4 copy.85
  157.6 8.8 %fusion.25 = f32[64,128,128]{2,1,0:T(8,128)S(1)} fusion(bf16[64,128,128]{2,1,0:T(8,128)(2,1)S(1)} %bitcast.147, f32[64,128,256]{2,1,0:T(8,128)S(1)} %bitcast.150, f32[64,128]{1,0:T(8,128)S(1)} %bitcast.164), kind=kOutput, calls=%fused_computation.36 | convolution fusion | flops 1612709888 | bytes 10518528 | tf_op jit(solution)/shard_map/qoa,qoi->qai/dot_general | solution.py:82
  166.3 2.4 copy.87
  168.8 9.4 %multiply_subtract_fusion.1 = f32[64,128,128]{2,1,0:T(8,128)S(1)} fusion(f32[64,128,256]{2,1,0:T(8,128)S(1)} %bitcast.150, bf16[64,128,128]{2,1,0:T(8,128)(2,1)S(1)} %bitcast.148, f32[64,128]{1,0:T(8,128)S(1)} %bitcast.165, f32[128,128]{1,0:T(8,128)S(1)} %fusion.106, f32[64]{0:T(128)S(1)} %slice_reduce_fusion), kind=kOutput, calls=%fused_computation.56 | convolution fusion | flops 1614807040 | bytes 10584576 | tf_op jit(solution)/shard_map/nsk,nsj->nkj/dot_general | solution.py:79
  178.2 2.5 copy.88
  180.8 45.7 %while.37 = (s32[]{:T(128)}, f32[4,128,128]{2,1,0:T(8,128)S(1)}, f32[4,128,128]{2,1,0:T(8,128)S(1)}, f32[16,4,128,128]{3,2,1,0:T(8,128)}, f32[16,4,128,128]{3,2,1,0:T(8,128)}, /*index=5*/s32[]{:T(128)}, s32[]{:T(128)}) while((s32[]{:T(128)}, f32[4,128,128]{2,1,0:T(8,128)S(1)}, f32[4,128,128]{2,1,0:T(8,128)S(1)}, ...), condition=%wide.region_3.4_spmd.clone, body=%wide.region_2.0_spmd.clone.sunk | while | flops 201457664 | bytes 2885207 | solution.py:122
  226.5 29.0 %while.35 = (s32[]{:T(128)}, f32[4,128,128]{2,1,0:T(8,128)S(1)}, f32[4,128,128]{2,1,0:T(8,128)S(1)}, f32[4,128,128]{2,1,0:T(8,128)S(1)}, s32[]{:T(128)}) while((s32[]{:T(128)}, f32[4,128,128]{2,1,0:T(8,128)S(1)}, f32[4,128,128]{2,1,0:T(8,128)S(1)}, f32[4,128,128]{2,1,0:T(8,128)S(1)}, s32[]{:T(128)}) %tuple.63), condition=%wide.region_5.6_spmd, body=%wide.region_4.5_spmd.sunk | while | flops 100728832 | bytes 2097253 | solution.py:128
  226.9 4.9 %collective-permute-start = (f32[4,128,128]{2,1,0:T(8,128)S(1)}, f32[4,128,128]{2,1,0:T(8,128)S(1)}, u32[]{:S(2)}, u32[]{:S(2)}) collective-permute-start(f32[4,128,128]{2,1,0:T(8,128)S(1)} %convolution_add_fusion.9), channel_id=1, source_target_pairs={{0,4},{4,8},{8,12},{1,5},{5,9},{9,13},{2,6},{6,10},{10,14},{3,7},{... | collective-permute-start | bytes 786440 | tf_op jit(solution)/shard_map/while/body/eval_jaxpr/ppermute | solution.py:15
  231.8 5.5 %collective-permute-done = f32[4,128,128]{2,1,0:T(8,128)S(1)} collective-permute-done((f32[4,128,128]{2,1,0:T(8,128)S(1)}, f32[4,128,128]{2,1,0:T(8,128)S(1)}, u32[]{:S(2)}, u32[]{:S(2)}) %collective-permute-start) | collective-permute-done | bytes 262176 | tf_op jit(solution)/shard_map/while/body/eval_jaxpr/ppermute | solution.py:15
  237.8 4.4 collective-permute-start
  242.2 4.7 collective-permute-done
  247.2 4.4 collective-permute-start
  251.6 3.9 collective-permute-done
  255.5 57.8 %while.36 = (s32[]{:T(128)}, f32[4,128,128]{2,1,0:T(8,128)S(1)}, f32[16,4,128,128]{3,2,1,0:T(8,128)}, f32[16,4,128,128]{3,2,1,0:T(8,128)}, f32[16,4,128,128]{3,2...) while((s32[]{:T(128)}, f32[4,128,128]{2,1,0:T(8,128)S(1)}, ...), condition=%wide.region_8.9_spmd, body=%wide.region_7.8_spmd.sunk | while | flops 201457664 | bytes 2623573 | solution.py:138
  262.7 2.1 fusion.181
  266.3 2.1 fusion.181
  269.9 2.2 fusion.181
  273.6 2.2 fusion.181
  277.2 2.1 fusion.181
  280.8 2.1 fusion.181
  284.4 2.1 fusion.181
  291.7 2.1 fusion.181
  295.3 2.1 fusion.181
  298.9 2.2 fusion.181
  309.7 2.1 fusion.181
  313.3 3.3 multiply_reduce_fusion.1
  316.6 5.5 %copy.73 = f32[16,128,4,128]{1,0,3,2:T(8,128)} copy(f32[16,128,4,128]{3,1,2,0:T(8,128)} %bitcast.154) | data formatting | bytes 8388608 | tf_op jit(solution)/shard_map/transpose | solution.py:139
  322.1 4.9 reshape.213
  327.0 4.3 convolution_bitcast_fusion
  332.1 6.0 %all-to-all-start.1 = ((s32[4,1,1]{2,1,0:T(1,128)}), s32[4,1,1]{2,1,0:T(1,128)S(1)}, u32[]{:S(2)}, u32[]{:S(2)}) async-start(s32[4,1,1]{2,1,0:T(1,128)} %copy.76), calls=%async_computation.2 | async-start | bytes 4096 | tf_op jit(solution)/shard_map/all_to_all | solution.py:176
  338.7 26.4 %reduce-scatter.2.cloned.1.call-done = f32[512,256]{1,0:T(8,128)} async-done(((f32[2048,256]{1,0:T(8,128)}), f32[512,256]{1,0:T(8,128)}) %reduce-scatter.2.cloned.1.call-update) | async-done | bytes 524304 | tf_op jit(solution)/shard_map/reduce_scatter | solution.py:153
  367.8 4.6 all-to-all-start
  372.8 14.1 %all-to-all-done = f32[4,128,256]{2,1,0:T(8,128)S(1)} async-done(((f32[4,128,256]{2,1,0:T(8,128)}), f32[4,128,256]{2,1,0:T(8,128)S(1)}, u32[]{:S(2)}, u32[]{:S(2)}) %all-to-all-start) | async-done | bytes 524320 | tf_op jit(solution)/shard_map/all_to_all | solution.py:175
  387.8 2.2 multiply_reduce_fusion.2
  389.9 16.4 %all_to_all.19 = f32[4,128,256]{2,1,0:T(8,128)S(1)} all-to-all(f32[4,128,256]{2,1,0:T(8,128)S(1)} %get-tuple-element.160), channel_id=1, replica_groups=mesh['grp'=2,'seq'=4,'head'=2,'tp'=2] {'seq'}, dimensions={0} | all-to-all | bytes 1048576 | tf_op jit(solution)/shard_map/all_to_all | solution.py:188
  408.7 30.7 %psum.15 = f32[]{:T(128)} all-reduce(f32[]{:T(128)} %select_reduce_fusion), channel_id=1, replica_groups=mesh['grp'=2,'seq'=4,'head'=2,'tp'=2] {'seq','head','tp'}, use_global_device_ids=true, to_apply=%region_22.23 | all-reduce | flops 1 | bytes 8 | tf_op jit(solution)/shard_map/psum | solution.py:202
  440.1 5.4 %multiply_reduce_fusion = (f32[2048,4]{0,1:T(4,128)S(1)}, f32[2048,4,128]{0,2,1:T(8,128)}) fusion(f32[2048,4,128]{0,2,1:T(8,128)} %reshape.213, f32[2048,4]{0,1:T(4,128)S(1)} %sqrt_bitcast_fusion, bf16[4,128,256]{2,1,0:T(8,128)(2,1)S(1)} %copy-done, bf16[2048,256]{1,0:T(8,128)(2,1)} %all-gather.2.cloned.1.call-done), kind=kOutput, calls=%fused_computation.48 | convolution fusion | flops 540008448 | bytes 9764864 | tf_op jit(solution)/shard_map/re,hde->rhd/dot_general | solution.py:196
  447.1 6.9 %subtract_divide_fusion = f32[2048,4,128]{0,2,1:T(8,128)} fusion(f32[2048,4,128]{0,2,1:T(8,128)} %get-tuple-element.162, f32[2048,4]{0,1:T(4,128)S(1)} %broadcast_multiply_fusion, f32[2048,4]{0,1:T(4,128)S(1)} %sqrt_bitcast_fusion, f32[2048,4,128]{0,2,1:T(8,128)} %reshape.213), kind=kLoop, calls=%fused_computation.47 | loop fusion | flops 4194304 | bytes 12648448 | tf_op jit(solution)/shard_map/div | solution.py:200
  453.9 5.2 %copy.77 = f32[2048,4,128]{2,1,0:T(4,128)} copy(f32[2048,4,128]{0,2,1:T(8,128)} %subtract_divide_fusion) | data formatting | bytes 8388608
  459.2 23.6 %all-reduce.2.cloned.1.call-done = f32[4,128,256]{2,1,0:T(8,128)} async-done(((f32[4,128,256]{2,1,0:T(8,128)}), f32[4,128,256]{2,1,0:T(8,128)}) %all-reduce.2.cloned.1.call-update) | async-done | bytes 524304 | tf_op jit(solution)/shard_map/psum | solution.py:199
  (187 shorter events, 96.8 us)
Async XLA Ops:
  7.2 319.8 %copy-start = (bf16[4,128,256]{2,1,0:T(8,128)(2,1)S(1)}, bf16[4,128,256]{2,1,0:T(8,128)(2,1)}, u32[]{:S(2)}) copy-start(bf16[4,128,256]{2,1,0:T(8,128)(2,1)} %param.20) | copy-start | bytes 786436
  7.2 5.2 %copy-start.4 = (bf16[2048,4,128]{2,1,0:T(4,128)(2,1)S(1)}, bf16[2048,4,128]{2,1,0:T(4,128)(2,1)}, u32[]{:S(2)}) copy-start(bf16[2048,4,128]{2,1,0:T(4,128)(2,1)} %param.16) | copy-start | bytes 6291460
  7.2 357.9 %reduce-scatter.2.cloned.1.call-start = ((), (), s32[]{:S(2)}) async-start(), calls=%async_computation.4 | async-start | bytes 2621440 | tf_op jit(solution)/shard_map/reduce_scatter | solution.py:153
  17.6 3.6 copy-start.9
  17.7 3.6 copy-start.10
  32.3 5.1 %copy-start.6 = (f32[64,128,128]{2,1,0:T(8,128)S(1)}, f32[64,128,128]{2,1,0:T(8,128)}, u32[]{:S(2)}) copy-start(f32[64,128,128]{2,1,0:T(8,128)} %fusion.118) | copy-start | bytes 12582916
  94.9 3.1 copy-start.7
  98.5 2.4 copy-start.5
  129.8 8.2 %copy-start.1 = (f32[64,128,256]{2,1,0:T(8,128)}, f32[64,128,256]{2,1,0:T(8,128)S(1)}, u32[]{:S(2)}) copy-start(f32[64,128,256]{2,1,0:T(8,128)S(1)} %fusion.22) | copy-start | bytes 25165828
  148.3 5.0 %copy-start.3 = (f32[64,128,128]{2,1,0:T(8,128)S(1)}, f32[64,128,128]{2,1,0:T(8,128)}, u32[]{:S(2)}) copy-start(f32[64,128,128]{2,1,0:T(8,128)} %fusion.33) | copy-start | bytes 12582916
  148.3 9.0 %slice-start = ((s8[8388608]{0:T(1024)(128)(4,1)}), s8[4194304]{0:T(1024)(128)(4,1)S(1)}, s32[]{:S(2)}) async-start(s8[8388608]{0:T(1024)(128)(4,1)} %bitcast.149), calls=%async_computation.7 | async-start | bytes 8388608
  153.3 4.3 slice-start.1
  226.9 10.5 %collective-permute-start = (f32[4,128,128]{2,1,0:T(8,128)S(1)}, f32[4,128,128]{2,1,0:T(8,128)S(1)}, u32[]{:S(2)}, u32[]{:S(2)}) collective-permute-start(f32[4,128,128]{2,1,0:T(8,128)S(1)} %convolution_add_fusion.9), channel_id=1, source_target_pairs={{0,4},{4,8},{8,12},{1,5},{5,9},{9,13},{2,6},{6,10},{10,14},{3,7},{... | collective-permute-start | bytes 786440 | tf_op jit(solution)/shard_map/while/body/eval_jaxpr/ppermute | solution.py:15
  237.8 9.1 %collective-permute-start = (f32[4,128,128]{2,1,0:T(8,128)S(1)}, f32[4,128,128]{2,1,0:T(8,128)S(1)}, u32[]{:S(2)}, u32[]{:S(2)}) collective-permute-start(f32[4,128,128]{2,1,0:T(8,128)S(1)} %convolution_add_fusion.9), channel_id=1, source_target_pairs={{0,4},{4,8},{8,12},{1,5},{5,9},{9,13},{2,6},{6,10},{10,14},{3,7},{... | collective-permute-start | bytes 786440 | tf_op jit(solution)/shard_map/while/body/eval_jaxpr/ppermute | solution.py:15
  247.2 8.3 %collective-permute-start = (f32[4,128,128]{2,1,0:T(8,128)S(1)}, f32[4,128,128]{2,1,0:T(8,128)S(1)}, u32[]{:S(2)}, u32[]{:S(2)}) collective-permute-start(f32[4,128,128]{2,1,0:T(8,128)S(1)} %convolution_add_fusion.9), channel_id=1, source_target_pairs={{0,4},{4,8},{8,12},{1,5},{5,9},{9,13},{2,6},{6,10},{10,14},{3,7},{... | collective-permute-start | bytes 786440 | tf_op jit(solution)/shard_map/while/body/eval_jaxpr/ppermute | solution.py:15
  327.0 4.3 copy-start.13
  327.0 11.1 %copy-start.11 = (s32[1,1,128]{2,1,0:T(1,128)S(1)}, s32[1,1,128]{2,1,0:T(1,128)}, u32[]{:S(2)}) copy-start(s32[1,1,128]{2,1,0:T(1,128)} %param.22) | copy-start | bytes 1540
  331.3 41.1 %copy-start.8 = (bf16[1,1,4,128,256]{4,3,2,1,0:T(8,128)(2,1)S(1)}, bf16[1,1,4,128,256]{4,3,2,1,0:T(8,128)(2,1)}, u32[]{:S(2)}) copy-start(bf16[1,1,4,128,256]{4,3,2,1,0:T(8,128)(2,1)} %param.21) | copy-start | bytes 786436
  332.1 35.7 %all-to-all-start.1 = ((s32[4,1,1]{2,1,0:T(1,128)}), s32[4,1,1]{2,1,0:T(1,128)S(1)}, u32[]{:S(2)}, u32[]{:S(2)}) async-start(s32[4,1,1]{2,1,0:T(1,128)} %copy.76), calls=%async_computation.2 | async-start | bytes 4096 | tf_op jit(solution)/shard_map/all_to_all | solution.py:176
  367.8 19.1 %all-to-all-start = ((f32[4,128,256]{2,1,0:T(8,128)}), f32[4,128,256]{2,1,0:T(8,128)S(1)}, u32[]{:S(2)}, u32[]{:S(2)}) async-start(f32[4,128,256]{2,1,0:T(8,128)} %bitcast.26), calls=%async_computation.1 | async-start | bytes 1048576 | tf_op jit(solution)/shard_map/all_to_all | solution.py:175
  372.4 67.6 %all-gather.2.cloned.1.call-start = ((), (), s32[]{:S(2)}) async-start(), calls=%async_computation.5 | async-start | bytes 1310720 | tf_op jit(solution)/shard_map/all_gather | solution.py:194
  407.9 74.8 %all-reduce.2.cloned.1.call-start = ((), (), s32[]{:S(2)}) async-start(), calls=%async_computation.6 | async-start | bytes 1048576 | tf_op jit(solution)/shard_map/psum | solution.py:199
  440.0 5.5 %copy-start.2 = (f32[2048,4,128]{0,2,1:T(8,128)S(1)}, f32[2048,4,128]{0,2,1:T(8,128)}, u32[]{:S(2)}) copy-start(f32[2048,4,128]{0,2,1:T(8,128)} %reshape.213) | copy-start | bytes 12582916
  440.0 5.5 %copy-start.12 = (bf16[2048,256]{1,0:T(8,128)(2,1)S(1)}, bf16[2048,256]{1,0:T(8,128)(2,1)}, u32[]{:S(2)}) copy-start(bf16[2048,256]{1,0:T(8,128)(2,1)} %all-gather.2.cloned.1.call-done) | copy-start | bytes 3145732
Sparse Core Ops, SparseCore 0:
  331.4 33.5 reduce-scatter.1
  408.1 14.9 all-gather.1
  447.2 35.5 all-reduce.1
where the time goes:
time: 500 us; the launch traced here: 493 us
  matrix products  247 us (49%)
  waiting for transfers between devices  78.2 us (16%)
  blocking collectives  47.1 us (9%)
  other arithmetic  41.2 us (8%)
  local copies, waits for them, and re-layouts  36.5 us (7%)
  starting transfers between devices  24.4 us (5%)
  between operations  16.3 us (3%)
    dot_general x63, matrix products, apply_map(): return jnp.einsum('hij,hjk->hik', first, second, precision=UPPER_LIMIT)  147 us
    dot_general x16, matrix products, emit(): jnp.einsum('aci,aie->ace', block_extent, recurrent_state, precision=UPPER...  34.3 us
    psum x1, blocking collectives, shards(): mean_kl = (lax.psum(kl_part, ('seq', 'head', 'tp')) / tokens_all).reshape(1)  30.7 us
    reduce_scatter x1, waiting for transfers between devices, shards(): lax.psum_scatter(jnp.einsum('rhd,hde->re', piece, router_weight, preferre...  26.4 us
    psum x1, waiting for transfers between devices, shards(): grad_router = lax.psum(weight_grad, 'seq')  23.6 us
    all_to_all x1, blocking collectives, shards(): lax.all_to_all(slot_grad, 'seq', split_axis=0, concat_axis=0, tiled=True)  16.4 us
    all_to_all x1, waiting for transfers between devices, shards(): lax.all_to_all(outgoing, 'seq', split_axis=0, concat_axis=0, tiled=True)  14.1 us
    ppermute x3, waiting for transfers between devices, shifted(): lax.ppermute(value, axis, [(source, source + steps) for source in range(l...  14 us
  transfers between devices with their start and end apart: 8, of which 6 were waited for; matrix products, arithmetic and copies ran while one was open for 3% of the time, Pallas kernels for 0%

commit v1 on v0

v1 whole, which is shorter than its diff:
```python
import functools

import jax
import jax.numpy as jnp
from jax import lax
from jax.experimental import pallas as pl
from jax.experimental.pallas import tpu as pltpu
from jax.sharding import PartitionSpec as P

BLOCK = 128
WIDTH = 128
BASE = 16
PAIR = 2
EXTRA = 16
LIMIT = 48 * 1024 * 1024
UPPER_LIMIT = lax.Precision.HIGHEST
F32 = jnp.float32
BF16 = jnp.bfloat16


def iota(shape, axis):
    return lax.broadcasted_iota(jnp.int32, shape, axis)


def mm(a, b):
    return jnp.dot(a, b, preferred_element_type=F32)


def mm_nt(a, b):
    return lax.dot_general(a, b, (((1,), (1,)), ((), ())), preferred_element_type=F32)


def mm_tn(a, b):
    return lax.dot_general(a, b, (((0,), (0,)), ((), ())), preferred_element_type=F32)


def split(x):
    high = x.astype(BF16)
    return high, (x - high.astype(F32)).astype(BF16)


def dot3(a, b):
    (ah, al), (bh, bl) = a, b
    return mm(jnp.concatenate([ah, al], axis=1), jnp.concatenate([bh, bh], axis=0)) + mm(ah, bl)


def delta_kernel(heads, q_ref, k_ref, v_ref, d_ref, r_ref, loc_ref, reach_ref, x_ref, wide):
    row, col = iota((BLOCK, BLOCK), 0), iota((BLOCK, BLOCK), 1)
    eye, closed, strict = row == col, row >= col, row > col

    @pl.when(pl.program_id(0) == 0)
    def _():
        for h in range(heads):
            x_ref[h] = jnp.concatenate(
                [jnp.zeros((WIDTH, WIDTH), F32), eye.astype(F32)], axis=1
            )

    wide[0] = q_ref[...].astype(F32)
    wide[1] = k_ref[...].astype(F32)
    wide[2] = v_ref[...].astype(F32)
    cells = [(b, h) for b in range(PAIR) for h in range(heads)]

    def unit(x):
        return (x * lax.rsqrt(jnp.sum(x * x, axis=-1, keepdims=True) + 1e-06)).astype(BF16)

    negs, rights, mixers, tails, gq, gends = [], [], [], [], [], []
    for b, h in cells:
        rows = pl.ds(b * BLOCK, BLOCK)
        q = unit(wide[0, rows, h, :])
        k = unit(wide[1, rows, h, :])
        v = wide[2, rows, h, :]
        decay = d_ref[h : h + 1, b * BLOCK : (b + 1) * BLOCK]
        rate = r_ref[h : h + 1, b * BLOCK : (b + 1) * BLOCK]
        cum = jnp.sum(jnp.where(closed, decay, 0.0), axis=1, keepdims=True)
        cum_row = jnp.sum(jnp.where(eye, cum, 0.0), axis=0, keepdims=True)
        rate_col = jnp.sum(jnp.where(eye, rate, 0.0), axis=1, keepdims=True)
        ratio = jnp.exp(jnp.where(closed, cum - cum_row, -1e30))
        gamma = jnp.exp(cum)
        end = cum[BLOCK - 1 : BLOCK, :]
        both = mm_nt(jnp.concatenate([k, q], axis=0), k)
        kf = k.astype(F32)
        negs.append(-(rate_col * jnp.where(strict, ratio * both[:BLOCK], 0.0)))
        rights.append(jnp.concatenate([rate_col * v, (rate_col * gamma) * kf], axis=1))
        mixers.append(ratio * both[BLOCK:])
        tails.append(jnp.transpose(kf * jnp.exp(end - cum)))
        gq.append(gamma * q.astype(F32))
        gends.append(jnp.exp(end))

    n = len(cells)
    same = (row // BASE) == (col // BASE)
    ident = eye.astype(F32)
    diag = [jnp.where(same, x, 0.0) for x in negs]
    inv = [ident + x for x in diag]
    power = [split(x) for x in diag]
    size = 2
    while size < BASE:
        power = [split(dot3(x, x)) for x in power]
        inv = [t + dot3(split(t), p) for t, p in zip(inv, power)]
        size *= 2
    size = BASE
    while size < BLOCK:
        level = ((row // (2 * size)) == (col // (2 * size))) & ((row // size) != (col // size))
        parts = [split(t) for t in inv]
        off = [split(jnp.where(level, x, 0.0)) for x in negs]
        half = [split(dot3(o, p)) for o, p in zip(off, parts)]
        inv = [t + dot3(p, m) for t, p, m in zip(inv, parts, half)]
        size *= 2
    solved = [split(dot3(split(t), split(r))) for t, r in zip(inv, rights)]
    mixed = [
        dot3(split(jnp.concatenate([m, t], axis=0)), s) for m, t, s in zip(mixers, tails, solved)
    ]
    maps = [
        split(
            jnp.concatenate(
                [gq[i] - mixed[i][:BLOCK, WIDTH:], gends[i] * ident - mixed[i][BLOCK:, WIDTH:]],
                axis=0,
            )
        )
        for i in range(n)
    ]
    states = [x_ref[h] for h in range(heads)]
    for i, (b, h) in enumerate(cells):
        rows = pl.ds(b * BLOCK, BLOCK)
        moved = dot3(maps[i], split(states[h]))
        loc_ref[h, rows, :] = moved[:BLOCK, :WIDTH] + mixed[i][:BLOCK, :WIDTH]
        reach_ref[h, rows, :] = moved[:BLOCK, WIDTH:]
        states[h] = jnp.concatenate(
            [moved[BLOCK:, :WIDTH] + mixed[i][BLOCK:, :WIDTH], moved[BLOCK:, WIDTH:]], axis=1
        )
    for h in range(heads):
        x_ref[h] = states[h]


def bounds(lens):
    tok = lens.shape[1]
    row, col = iota((tok, tok), 0), iota((tok, tok), 1)
    start = jnp.sum(jnp.where(col < row, lens, 0.0), axis=1, keepdims=True)
    own = jnp.sum(jnp.where(col == row, lens, 0.0), axis=1, keepdims=True)
    return start, own, row == col


def pool_kernel(heads, lens_ref, loc_ref, reach_ref, s_ref, w_ref, out_ref, sum_ref, log_ref):
    region = loc_ref.shape[1]
    tok = sum_ref.shape[0]
    lens = lens_ref[pl.ds(pl.program_id(0), 1), :].astype(F32)
    start, own, _ = bounds(lens)
    place = iota((tok, region), 1).astype(F32)
    member = ((place >= start) & (place < start + own)).astype(F32).astype(BF16)
    total = jnp.zeros((tok, w_ref.shape[2]), F32)
    for h in range(heads):
        head = loc_ref[h] + dot3(split(reach_ref[h]), split(s_ref[h]))
        out_ref[h] = head
        inverse = lax.rsqrt(jnp.mean(head * head, axis=-1, keepdims=True) + 1e-06)
        summed = mm(member, (head * inverse).astype(BF16))
        sum_ref[:, h * WIDTH : (h + 1) * WIDTH] = summed
        high, low = split(summed)
        total = total + mm(high, w_ref[h]) + mm(low, w_ref[h])
    log_ref[...] = total


def log_probs(x):
    shifted_x = x - jnp.max(x, axis=-1, keepdims=True)
    return shifted_x - jnp.log(jnp.sum(jnp.exp(shifted_x), axis=-1, keepdims=True))


def loss_kernel(cap, lens_ref, own_ref, row_ref, teach_ref, log_ref, g_ref):
    tok = log_ref.shape[0]
    experts = log_ref.shape[1]
    _, own, _ = bounds(lens_ref[...].astype(F32))
    row, col = iota((tok, tok), 0), iota((tok, tok), 1)
    earlier = ((own_ref[...] == row_ref[...]) & (col < row)).astype(F32)
    slot = jnp.sum(earlier, axis=1, keepdims=True)
    target = own_ref[...].astype(F32) * cap + slot
    count = teach_ref.shape[0]
    pick = (iota((tok, count), 1).astype(F32) == target).astype(F32).astype(BF16)
    teacher_lp = log_probs(mm(pick, teach_ref[...]))
    student_lp = log_probs(log_ref[...] / own)
    prob = jnp.exp(teacher_lp)
    kl = jnp.sum(prob * (teacher_lp - student_lp), axis=-1, keepdims=True)
    kl = jnp.sum(kl, axis=0, keepdims=True)
    g_ref[0:tok, :] = ((jnp.exp(student_lp) - prob) / own).astype(BF16)
    high, rest = split(kl)
    low = kl - high.astype(F32) - rest.astype(F32)
    line = iota((EXTRA, experts), 0)
    g_ref[tok : tok + EXTRA, :] = jnp.where(
        line == 0, high.astype(F32), jnp.where(line == 1, rest.astype(F32), jnp.where(line == 2, low, 0.0))
    ).astype(BF16)


def router_kernel(regions, sum_ref, g_ref, out_ref):
    tok = sum_ref.shape[0] // regions
    wide = sum_ref.shape[1]
    total = jnp.zeros((wide, g_ref.shape[1]), F32)
    kl = jnp.zeros((EXTRA, g_ref.shape[1]), F32)
    for r in range(regions):
        first = r * (tok + EXTRA)
        g = g_ref[first : first + tok, :]
        high, low = split(sum_ref[r * tok : (r + 1) * tok, :])
        total = total + mm_tn(jnp.concatenate([high, low], axis=0), jnp.concatenate([g, g], axis=0))
        kl = kl + g_ref[first + tok : first + tok + EXTRA, :].astype(F32)
    out_ref[0:wide, :] = total
    out_ref[wide : wide + 8, :] = jnp.broadcast_to(
        jnp.sum(kl, axis=0, keepdims=True), (8, g_ref.shape[1])
    )


def heads_kernel(heads, lens_ref, head_ref, g_ref, w_ref, out_ref):
    region = head_ref.shape[1]
    tok = lens_ref.shape[1]
    lens = lens_ref[pl.ds(pl.program_id(0), 1), :].astype(F32)
    start, _, eye = bounds(lens)
    start_row = jnp.sum(jnp.where(eye, start, 0.0), axis=0, keepdims=True)
    place = iota((region, tok), 0).astype(F32)
    member = ((place >= start_row) & (place < start_row + lens)).astype(F32).astype(BF16)
    g = g_ref[0:tok, :]
    for h in range(heads):
        high, low = split(mm_nt(g, w_ref[h]))
        grad = mm(member, high) + mm(member, low)
        head = head_ref[h]
        inverse = lax.rsqrt(jnp.mean(head * head, axis=-1, keepdims=True) + 1e-06)
        unit = head * inverse
        mean = jnp.mean(grad * unit, axis=-1, keepdims=True)
        out_ref[:, h, :] = (grad - unit * mean) * inverse


def shifted(value, axis, steps):
    count = lax.axis_size(axis)
    return lax.ppermute(value, axis, [(source, source + steps) for source in range(count - steps)])


def params():
    return pltpu.CompilerParams(vmem_limit_bytes=LIMIT)


def cost(flops, size):
    return pl.CostEstimate(flops=flops, bytes_accessed=size, transcendentals=0)


def shards(
    queries,
    key_rows,
    values,
    log_decay,
    write_rate,
    router_weight,
    teacher_logits,
    span_length,
    span_owner,
):
    rows, heads, width = queries.shape
    regions = lax.axis_size(("head", "tp"))
    region = rows // regions
    lens = span_length.reshape(1, -1)
    tok = lens.shape[1]
    n_seq = lax.axis_size("seq")
    cap = teacher_logits.shape[3]
    experts = teacher_logits.shape[4]
    sds = jax.ShapeDtypeStruct

    teacher = lax.all_to_all(
        teacher_logits.reshape(n_seq, cap, experts), "seq", split_axis=0, concat_axis=0, tiled=True
    ).reshape(n_seq * cap, experts)
    lens_all = lax.all_gather(lens, ("head", "tp"), axis=0, tiled=True)

    step = PAIR * BLOCK
    whole = lambda shape: pl.BlockSpec(shape, lambda i: (0,) * len(shape))
    by_rows = pl.BlockSpec((step, heads, width), lambda i: (i, 0, 0))
    by_lane = pl.BlockSpec((heads, step), lambda i: (0, i))
    by_head = pl.BlockSpec((heads, step, width), lambda i: (0, i, 0))
    local, reach, ends = pl.pallas_call(
        functools.partial(delta_kernel, heads),
        grid=(rows // step,),
        in_specs=[by_rows, by_rows, by_rows, by_lane, by_lane],
        out_specs=[by_head, by_head, whole((heads, width, 2 * width))],
        out_shape=[
            sds((heads, rows, width), F32),
            sds((heads, rows, width), F32),
            sds((heads, width, 2 * width), F32),
        ],
        scratch_shapes=[pltpu.VMEM((3, step, heads, width), F32)],
        compiler_params=params(),
        cost_estimate=cost(30_000_000_000, 20_000_000),
        name="delta",
    )(queries, key_rows, values, log_decay, write_rate)
    dev_add, dev_map = ends[:, :, :width], ends[:, :, width:]

    state = shifted(dev_add, "seq", 1) if n_seq > 1 else jnp.zeros_like(dev_add)
    for _ in range(n_seq - 2):
        moved = jnp.einsum("hij,hjk->hik", dev_map, state, precision=UPPER_LIMIT) + dev_add
        state = shifted(moved, "seq", 1)

    by_region = pl.BlockSpec((heads, region, width), lambda i: (0, i, 0))
    head_out, sums, partial = pl.pallas_call(
        functools.partial(pool_kernel, heads),
        grid=(regions,),
        in_specs=[
            whole((regions, tok)),
            by_region,
            by_region,
            whole((heads, width, width)),
            whole((heads, width, experts)),
        ],
        out_specs=[
            by_region,
            pl.BlockSpec((tok, heads * width), lambda i: (i, 0)),
            pl.BlockSpec((tok, experts), lambda i: (i, 0)),
        ],
        out_shape=[
            sds((heads, rows, width), F32),
            sds((regions * tok, heads * width), F32),
            sds((regions * tok, experts), F32),
        ],
        compiler_params=params(),
        cost_estimate=cost(3_000_000_000, 16_000_000),
        name="pool",
    )(lens_all, local, reach, state, router_weight)

    summed = lax.psum_scatter(partial, ("head", "tp"), scatter_dimension=0, tiled=True)
    grads = pl.pallas_call(
        functools.partial(loss_kernel, cap),
        out_shape=sds((tok + EXTRA, experts), BF16),
        compiler_params=params(),
        name="loss",
    )(lens, span_owner.reshape(tok, 1), span_owner.reshape(1, tok), teacher, summed)
    gathered = lax.all_gather(grads, ("head", "tp"), axis=0, tiled=True)

    router = pl.pallas_call(
        functools.partial(router_kernel, regions),
        out_shape=sds((heads * width + 8, experts), F32),
        compiler_params=params(),
        cost_estimate=cost(300_000_000, 2_000_000),
        name="router",
    )(sums, gathered)
    router = lax.psum(router, "seq")
    grad_heads = pl.pallas_call(
        functools.partial(heads_kernel, heads),
        grid=(regions,),
        in_specs=[
            whole((regions, tok)),
            by_region,
            pl.BlockSpec((tok + EXTRA, experts), lambda i: (i, 0)),
            whole((heads, width, experts)),
        ],
        out_specs=pl.BlockSpec((region, heads, width), lambda i: (i, 0, 0)),
        out_shape=sds((rows, heads, width), F32),
        compiler_params=params(),
        cost_estimate=cost(3_000_000_000, 12_000_000),
        name="heads",
    )(lens_all, head_out, gathered, router_weight)
    grad_router = router[: heads * width].reshape(heads, width, experts)
    mean_kl = router[heads * width, :1] / (tok * n_seq * regions)
    return (grad_router, grad_heads, mean_kl)


def solution(mesh):
    placed = (
        P(("grp", "seq"), ("head", "tp"), None),
        P(("grp", "seq"), ("head", "tp"), None),
        P(("grp", "seq"), ("head", "tp"), None),
        P(("head", "tp"), ("grp", "seq")),
        P(("head", "tp"), ("grp", "seq")),
        P(("head", "tp"), None, None),
        P(("grp", "seq"), ("head", "tp"), None, None, None),
        P(("grp", "seq"), ("head", "tp"), None),
        P(("grp", "seq"), ("head", "tp"), None, None),
    )
    return jax.shard_map(
        shards,
        mesh=mesh,
        in_specs=placed,
        out_specs=(
            P(("grp", "head", "tp"), None, None),
            P(("grp", "seq"), ("head", "tp"), None),
            P("grp"),
        ),
        check_vma=False,
    )
```

time: 500 us -> 191 us (0.38); the launches traced: 493 us -> 190 us
  matrix products: 247 us -> 0.79 us
  Pallas kernels: 0 us -> 74.9 us
  other arithmetic: 41.2 us -> 0 us
  blocking collectives: 47.1 us -> 10.9 us
  local copies, waits for them, and re-layouts: 36.5 us -> 11 us
  waiting for transfers between devices: 78.2 us -> 58.2 us
  starting transfers between devices: 24.4 us -> 18.4 us
    dot_general x93 -> x2, matrix products: 247 us -> 0.79 us  [shards(): jnp.einsum('hij,hjk->hik', dev_map, state, precision=UPPER_LIMIT) + dev_add]
    pallas_call x0 -> x5, Pallas kernels: none -> 74.9 us  [the longest x1 54.6 us: shards(): pl.pallas_call(functools.partial(delta_kernel, heads), grid=(rows // step...]
    psum x1 -> x0, blocking collectives: 30.7 us -> none  [shards(): mean_kl = (lax.psum(kl_part, ('seq', 'head', 'tp')) / tokens_all).reshape(1)]
    reshape x7 -> x1, local copies, waits for them, and re-layouts: 19.4 us -> 0.11 us  [shards(): span_owner.reshape(tok, 1)]
    reduce_scatter x1, waiting for transfers between devices: 26.4 us -> 9.54 us  [shards(): lax.psum_scatter(partial, ('head', 'tp'), scatter_dimension=0, tiled=True)]
    all_to_all x1 -> x0, blocking collectives: 16.4 us -> none  [shards(): lax.all_to_all(slot_grad, 'seq', split_axis=0, concat_axis=0, tiled=True)]
    reduce_sum x8 -> x0, other arithmetic: 15.4 us -> none  [the longest x2 8.48 us: unit_rows(): jnp.sum(array * array, axis=-1, keepdims=True) + 1e-06]
    all_gather x0 -> x2, blocking collectives: none -> 10.9 us  [the longest x1 5.88 us: shards(): gathered = lax.all_gather(grads, ('head', 'tp'), axis=0, tiled=True)]
  transfers between devices with their start and end apart: 8 -> 6, of which waited for: 6 -> 5; matrix products, arithmetic and copies ran while one was open for 3% -> 0% of each run, Pallas kernels for 0% -> 4%
where the time goes in v1:
time: 191 us; the launch traced here: 190 us
  Pallas kernels  74.9 us (39%)
  waiting for transfers between devices  58.2 us (30%)
  starting transfers between devices  18.4 us (10%)
  between operations  15.9 us (8%)
  local copies, waits for them, and re-layouts  11 us (6%)
  blocking collectives  10.9 us (6%)
    pallas_call x1, Pallas kernels, shards(): pl.pallas_call(functools.partial(delta_kernel, heads), grid=(rows // step...  54.6 us
    psum x1, waiting for transfers between devices, shards(): router = lax.psum(router, 'seq')  29.9 us
    ppermute x3, starting transfers between devices, shifted(): lax.ppermute(value, axis, [(source, source + steps) for source in range(c...  13.7 us
    pallas_call x1, Pallas kernels, shards(): pl.pallas_call(functools.partial(pool_kernel, heads), grid=(regions,), in...  11.7 us
    ppermute x3, waiting for transfers between devices, shifted(): lax.ppermute(value, axis, [(source, source + steps) for source in range(c...  10.2 us
    reduce_scatter x1, waiting for transfers between devices, shards(): lax.psum_scatter(partial, ('head', 'tp'), scatter_dimension=0, tiled=True)  9.54 us
    all_to_all x1, waiting for transfers between devices, shards(): lax.all_to_all(teacher_logits.reshape(n_seq, cap, experts), 'seq', split_...  8.51 us
    unnamed x18, local copies, waits for them, and re-layouts  7.79 us
  transfers between devices with their start and end apart: 6, of which 5 were waited for; matrix products, arithmetic and copies ran while one was open for 0% of the time, Pallas kernels for 4%

profile of v1, /device:TPU:0, one launch (start us, length us, event | category | flops | bytes accessed | tf_op | source)
XLA Modules:
  0.0 190.0 jit_solution(15177005095465315387)
XLA Ops:
  7.2 0.0 copy-start.2
  7.2 0.0 reduce-scatter.2.cloned.1.call-start
  7.2 0.0 copy-start.3
  7.2 1.6 copy-done.3
  8.8 0.0 copy-start.4
  8.8 1.6 copy-done.4
  10.4 0.0 copy-start.6
  10.4 0.8 copy-done.6
  11.2 0.0 copy-start.7
  11.2 0.8 copy-done.7
  11.9 0.0 copy-start.5
  11.9 54.6 %delta.1 = (f32[4,2048,128]{2,1,0:T(8,128)}, f32[4,2048,128]{2,1,0:T(8,128)}, f32[4,128,256]{2,1,0:T(8,128)S(1)}) custom-call(bf16[2048,4,128]{2,1,0:T(4,128)(2,1)S(1)} %copy-done.3, bf16[2048,4,128]{2,1,0:T(4,128)(2,1)S(1)} %copy-done.4, bf16[2048,4,128]{2,1,0:T(4,128)(2,1)} %v_ref.1, f32[4,2048]{1,0:T(4,128)S(1)} %copy-done.6, f32[4,2048]{1,0:T(4,128)S(1)} %copy-done.7), custom_call_target="tpu_custom_call" | custom-call | flops 30000001024 | bytes 20000000 | tf_op jit(solution)/shard_map/delta/pallas_call | solution.py:270
  66.6 4.9 %collective-permute-start = (f32[4,128,128]{2,1,0:T(8,128)S(1)}, f32[4,128,128]{2,1,0:T(8,128)S(1)}, u32[]{:S(2)}, u32[]{:S(2)}) collective-permute-start(f32[4,128,128]{2,1,0:T(8,128)S(1)} %slice.13), channel_id=1, source_target_pairs={{0,4},{4,8},{8,12},{1,5},{5,9},{9,13},{2,6},{6,10},{10,14},{3,7},{... | collective-permute-start | bytes 786440 | tf_op jit(solution)/shard_map/ppermute | solution.py:228
  71.5 5.5 %collective-permute-done = f32[4,128,128]{2,1,0:T(8,128)S(1)} collective-permute-done((f32[4,128,128]{2,1,0:T(8,128)S(1)}, f32[4,128,128]{2,1,0:T(8,128)S(1)}, u32[]{:S(2)}, u32[]{:S(2)}) %collective-permute-start) | collective-permute-done | bytes 262176 | tf_op jit(solution)/shard_map/ppermute | solution.py:228
  77.0 0.4 convolution_add_fusion.1
  77.4 4.4 %collective-permute-start.1 = (f32[4,128,128]{2,1,0:T(8,128)S(1)}, f32[4,128,128]{2,1,0:T(8,128)S(1)}, u32[]{:S(2)}, u32[]{:S(2)}) collective-permute-start(f32[4,128,128]{2,1,0:T(8,128)S(1)} %convolution_add_fusion.1), channel_id=1, source_target_pairs={{0,4},{4,8},{8,12},{1,5},{5,9},{9,13},{2,6},{6,10},{10,14},{3,7},{... | collective-permute-start | bytes 786440 | tf_op jit(solution)/shard_map/ppermute | solution.py:228
  81.9 4.7 %collective-permute-done.1 = f32[4,128,128]{2,1,0:T(8,128)S(1)} collective-permute-done((f32[4,128,128]{2,1,0:T(8,128)S(1)}, f32[4,128,128]{2,1,0:T(8,128)S(1)}, u32[]{:S(2)}, u32[]{:S(2)}) %collective-permute-start.1) | collective-permute-done | bytes 262176 | tf_op jit(solution)/shard_map/ppermute | solution.py:228
  86.5 0.4 convolution_add_fusion
  86.9 4.4 %collective-permute-start.2 = (f32[4,128,128]{2,1,0:T(8,128)S(1)}, f32[4,128,128]{2,1,0:T(8,128)S(1)}, u32[]{:S(2)}, u32[]{:S(2)}) collective-permute-start(f32[4,128,128]{2,1,0:T(8,128)S(1)} %convolution_add_fusion), channel_id=1, source_target_pairs={{0,4},{4,8},{8,12},{1,5},{5,9},{9,13},{2,6},{6,10},{10,14},{3,7},{... | collective-permute-start | bytes 786440 | tf_op jit(solution)/shard_map/ppermute | solution.py:228
  91.3 0.0 copy-done.2
  91.3 5.0 %all-gather = s32[4,1,128]{2,1,0:T(1,128)S(1)} all-gather(s32[1,1,128]{2,1,0:T(1,128)S(1)} %copy-done.2), channel_id=2, replica_groups=mesh['grp'=2,'seq'=4,'head'=2,'tp'=2] {'head','tp'}, dimensions={0}, use_global_device_ids=true | all-gather | bytes 2560 | tf_op jit(solution)/shard_map/all_gather | solution.py:263
  96.4 0.0 collective-permute-done.2.s_ref
  96.4 0.0 copy-done.5
  96.4 0.0 copy-start.1
  96.4 11.7 %pool.1 = (f32[4,2048,128]{2,1,0:T(8,128)}, f32[512,512]{1,0:T(8,128)S(1)}, f32[512,256]{1,0:T(8,128)}) custom-call(s32[4,128]{1,0:T(4,128)S(1)} %bitcast.11, f32[4,2048,128]{2,1,0:T(8,128)} %get-tuple-element.9.loc_ref, f32[4,2048,128]{2,1,0:T(8,128)} %get-tuple-element.10.reach_ref, f32[4,128,128]{2,1,0:T(8,128)S(1)} %collective-permute-done.2.s_ref, ...), custom_call_target="tpu_custom_call" | custom-call | flops 3000000000 | bytes 16000000 | tf_op jit(solution)/shard_map/pool/pallas_call | solution.py:293
  108.0 0.0 reduce-scatter.2.cloned.1.call-update
  108.1 4.6 %all-to-all-start = ((bf16[4,128,256]{2,1,0:T(8,128)(2,1)}), bf16[4,128,256]{2,1,0:T(8,128)(2,1)S(1)}, u32[]{:S(2)}, u32[]{:S(2)}) async-start(bf16[4,128,256]{2,1,0:T(8,128)(2,1)} %bitcast.4), calls=%async_computation | async-start | bytes 524288 | tf_op jit(solution)/shard_map/all_to_all | solution.py:260
  112.6 0.0 all-reduce.2.cloned.1.call-start
  112.6 0.0 copy-done.1
  112.7 0.1 copy.14.own_ref
  112.8 8.5 %all-to-all-done = bf16[4,128,256]{2,1,0:T(8,128)(2,1)S(1)} async-done(((bf16[4,128,256]{2,1,0:T(8,128)(2,1)}), bf16[4,128,256]{2,1,0:T(8,128)(2,1)S(1)}, u32[]{:S(2)}, u32[]{:S(2)}) %all-to-all-start) | async-done | bytes 262176 | tf_op jit(solution)/shard_map/all_to_all | solution.py:260
  121.3 9.5 %reduce-scatter.2.cloned.1.call-done.log_ref = f32[128,256]{1,0:T(8,128)} async-done(((f32[512,256]{1,0:T(8,128)}), f32[128,256]{1,0:T(8,128)}) %reduce-scatter.2.cloned.1.call-update) | async-done | bytes 131088 | tf_op jit(solution)/shard_map/reduce_scatter | solution.py:318
  130.8 0.0 copy-start
  130.8 0.9 copy-done
  131.7 0.7 loss.1
  132.4 5.9 %all_gather.7.g_ref = bf16[576,256]{1,0:T(8,128)(2,1)S(1)} all-gather(bf16[144,256]{1,0:T(8,128)(2,1)S(1)} %loss.1), channel_id=1, replica_groups=mesh['grp'=2,'seq'=4,'head'=2,'tp'=2] {'head','tp'}, dimensions={0}, use_global_device_ids=true | all-gather | bytes 368640 | tf_op jit(solution)/shard_map/all_gather | solution.py:325
  138.3 1.3 router.1
  139.6 0.0 all-reduce.2.cloned.1.call-update
  139.6 0.0 copy-start.8
  139.6 2.2 %copy-done.8 = f32[4,2048,128]{2,1,0:T(8,128)S(1)} copy-done((f32[4,2048,128]{2,1,0:T(8,128)S(1)}, f32[4,2048,128]{2,1,0:T(8,128)}, u32[]{:S(2)}) %copy-start.8) | copy-done | bytes 4194328
  141.8 6.7 %heads.1 = f32[2048,4,128]{2,1,0:T(4,128)} custom-call(s32[4,128]{1,0:T(4,128)S(1)} %bitcast.12, f32[4,2048,128]{2,1,0:T(8,128)S(1)} %copy-done.8, bf16[576,256]{1,0:T(8,128)(2,1)S(1)} %all_gather.7.g_ref, bf16[4,128,256]{2,1,0:T(8,128)(2,1)S(1)} %copy-done.5), custom_call_target="tpu_custom_call" | custom-call | flops 3000000000 | bytes 12000000 | tf_op jit(solution)/shard_map/heads/pallas_call | solution.py:335
  148.4 29.9 %all-reduce.2.cloned.1.call-done = f32[520,256]{1,0:T(8,128)} async-done(((f32[520,256]{1,0:T(8,128)}), f32[520,256]{1,0:T(8,128)}) %all-reduce.2.cloned.1.call-update) | async-done | bytes 532496 | tf_op jit(solution)/shard_map/psum | solution.py:334
  178.3 1.2 slice.17
  180.2 1.9 slice.16
  (1 shorter events, 0.0 us)
Async XLA Ops:
  7.2 84.2 %copy-start.2 = (s32[1,1,128]{2,1,0:T(1,128)S(1)}, s32[1,1,128]{2,1,0:T(1,128)}, u32[]{:S(2)}) copy-start(s32[1,1,128]{2,1,0:T(1,128)} %param.16) | copy-start | bytes 1540
  7.2 123.6 %reduce-scatter.2.cloned.1.call-start = ((), (), s32[]{:S(2)}) async-start(), calls=%async_computation.2 | async-start | bytes 655360 | tf_op jit(solution)/shard_map/reduce_scatter | solution.py:318
  7.2 1.6 copy-start.3
  8.8 1.6 copy-start.4
  10.4 0.8 copy-start.6
  11.2 0.8 copy-start.7
  11.9 84.5 %copy-start.5 = (bf16[4,128,256]{2,1,0:T(8,128)(2,1)S(1)}, bf16[4,128,256]{2,1,0:T(8,128)(2,1)}, u32[]{:S(2)}) copy-start(bf16[4,128,256]{2,1,0:T(8,128)(2,1)} %w_ref.3) | copy-start | bytes 786436
  66.6 10.5 %collective-permute-start = (f32[4,128,128]{2,1,0:T(8,128)S(1)}, f32[4,128,128]{2,1,0:T(8,128)S(1)}, u32[]{:S(2)}, u32[]{:S(2)}) collective-permute-start(f32[4,128,128]{2,1,0:T(8,128)S(1)} %slice.13), channel_id=1, source_target_pairs={{0,4},{4,8},{8,12},{1,5},{5,9},{9,13},{2,6},{6,10},{10,14},{3,7},{... | collective-permute-start | bytes 786440 | tf_op jit(solution)/shard_map/ppermute | solution.py:228
  77.4 9.1 %collective-permute-start.1 = (f32[4,128,128]{2,1,0:T(8,128)S(1)}, f32[4,128,128]{2,1,0:T(8,128)S(1)}, u32[]{:S(2)}, u32[]{:S(2)}) collective-permute-start(f32[4,128,128]{2,1,0:T(8,128)S(1)} %convolution_add_fusion.1), channel_id=1, source_target_pairs={{0,4},{4,8},{8,12},{1,5},{5,9},{9,13},{2,6},{6,10},{10,14},{3,7},{... | collective-permute-start | bytes 786440 | tf_op jit(solution)/shard_map/ppermute | solution.py:228
  86.9 9.5 %collective-permute-start.2 = (f32[4,128,128]{2,1,0:T(8,128)S(1)}, f32[4,128,128]{2,1,0:T(8,128)S(1)}, u32[]{:S(2)}, u32[]{:S(2)}) collective-permute-start(f32[4,128,128]{2,1,0:T(8,128)S(1)} %convolution_add_fusion), channel_id=1, source_target_pairs={{0,4},{4,8},{8,12},{1,5},{5,9},{9,13},{2,6},{6,10},{10,14},{3,7},{... | collective-permute-start | bytes 786440 | tf_op jit(solution)/shard_map/ppermute | solution.py:228
  96.4 16.3 %copy-start.1 = (s32[1,1,128,1]{2,3,1,0:T(1,128)S(1)}, s32[1,1,128,1]{2,3,1,0:T(1,128)}, u32[]{:S(2)}) copy-start(s32[1,1,128,1]{2,3,1,0:T(1,128)} %param.17) | copy-start | bytes 1540
  108.1 13.2 %all-to-all-start = ((bf16[4,128,256]{2,1,0:T(8,128)(2,1)}), bf16[4,128,256]{2,1,0:T(8,128)(2,1)S(1)}, u32[]{:S(2)}, u32[]{:S(2)}) async-start(bf16[4,128,256]{2,1,0:T(8,128)(2,1)} %bitcast.4), calls=%async_computation | async-start | bytes 524288 | tf_op jit(solution)/shard_map/all_to_all | solution.py:260
  112.6 65.7 %all-reduce.2.cloned.1.call-start = ((), (), s32[]{:S(2)}) async-start(), calls=%async_computation.3 | async-start | bytes 1064960 | tf_op jit(solution)/shard_map/psum | solution.py:334
  130.8 0.9 copy-start
  139.6 2.2 %copy-start.8 = (f32[4,2048,128]{2,1,0:T(8,128)S(1)}, f32[4,2048,128]{2,1,0:T(8,128)}, u32[]{:S(2)}) copy-start(f32[4,2048,128]{2,1,0:T(8,128)} %get-tuple-element.14.head_ref) | copy-start | bytes 12582916
Sparse Core Ops, SparseCore 0:
  108.2 22.5 reduce-scatter.1
  139.7 38.5 all-reduce.1

commit v2 on v1

--- a/solution.py
+++ b/solution.py
@@ -163,33 +163,156 @@
     return shifted_x - jnp.log(jnp.sum(jnp.exp(shifted_x), axis=-1, keepdims=True))
 
 
-def loss_kernel(cap, lens_ref, own_ref, row_ref, teach_ref, log_ref, g_ref):
-    tok = log_ref.shape[0]
+MESH = pl.DeviceIdType.MESH
+
+
+def tile_place(index):
+    count = lax.axis_size("tp")
+    return {"head": index // count, "tp": lax.rem(index, count)}
+
+
+def signal(barrier, device):
+    pl.semaphore_signal(barrier, inc=1, device_id=device, device_id_type=MESH)
+
+
+def send(source, target, sems, slot, device):
+    return pltpu.make_async_remote_copy(
+        src_ref=source,
+        dst_ref=target,
+        send_sem=sems.at[0, slot],
+        recv_sem=sems.at[1, slot],
+        device_id=device,
+        device_id_type=MESH,
+    )
+
+
+def relay_kernel(heads, n_seq, regions, ends_ref, lens_ref, s_ref, all_ref, came, gone, lbuf, sems, lsems):
+    me = lax.axis_index("seq")
+    tile = lax.axis_index("head") * lax.axis_size("tp") + lax.axis_index("tp")
+    barrier = pltpu.get_barrier_semaphore()
+
+    for o in (1, n_seq - 1):
+        signal(barrier, {"seq": lax.rem(me + o, n_seq)})
+    for o in range(1, regions):
+        signal(barrier, tile_place(lax.rem(tile + o, regions)))
+    pl.semaphore_wait(barrier, regions + 1)
+
+    def hop(h):
+        return send(gone.at[h], came.at[h], sems, h, {"seq": lax.rem(me + 1, n_seq)})
+
+    @pl.when(me == 0)
+    def _():
+        for h in range(heads):
+            gone[h] = ends_ref[h, :, :WIDTH]
+            hop(h).start()
+        s_ref[...] = jnp.zeros_like(s_ref)
+
+    lens_copies = [
+        send(lens_ref, lbuf.at[tile], lsems, o, tile_place(lax.rem(tile + o, regions)))
+        for o in range(1, regions)
+    ]
+    for copy in lens_copies:
+        copy.start()
+    lbuf[tile] = lens_ref[...]
+
+    @pl.when(me > 0)
+    def _():
+        for h in range(heads):
+            hop(h).wait_recv()
+            state = came[h]
+            s_ref[h] = state
+
+            @pl.when(me < n_seq - 1)
+            def _():
+                gone[h] = dot3(split(ends_ref[h, :, WIDTH:]), split(state)) + ends_ref[h, :, :WIDTH]
+                hop(h).start()
+
+    for copy in lens_copies:
+        copy.wait()
+    for r in range(regions):
+        all_ref[r : r + 1, :] = lbuf[r, 0:1, :]
+
+    @pl.when(me < n_seq - 1)
+    def _():
+        for h in range(heads):
+            hop(h).wait_send()
+
+
+def loss_kernel(
+    cap, n_seq, regions, lens_ref, own_ref, row_ref, teach_ref, log_ref, out_ref, tbuf, lbuf, gbuf, tsems, lsems, gsems
+):
     experts = log_ref.shape[1]
+    tok = log_ref.shape[0] // regions
+    me = lax.axis_index("seq")
+    tile = lax.axis_index("head") * lax.axis_size("tp") + lax.axis_index("tp")
+    barrier = pltpu.get_barrier_semaphore()
+    for o in range(1, regions):
+        signal(barrier, tile_place(lax.rem(tile + o, regions)))
+    for o in range(1, n_seq):
+        signal(barrier, {"seq": lax.rem(me + o, n_seq)})
+    pl.semaphore_wait(barrier, regions + n_seq - 2)
+    logs, teachers = [], []
+    for o in range(1, regions):
+        peer = lax.rem(tile + o, regions)
+        part = log_ref.at[pl.ds(pl.multiple_of(peer * tok, tok), tok), :]
+        logs.append(send(part, lbuf.at[o], lsems, o, tile_place(peer)))
+        logs[-1].start()
+    for o in range(1, n_seq):
+        peer = lax.rem(me + o, n_seq)
+        teachers.append(send(teach_ref.at[peer], tbuf.at[me], tsems, o, {"seq": peer}))
+        teachers[-1].start()
+    tbuf[me] = teach_ref[me]
+
     _, own, _ = bounds(lens_ref[...].astype(F32))
     row, col = iota((tok, tok), 0), iota((tok, tok), 1)
     earlier = ((own_ref[...] == row_ref[...]) & (col < row)).astype(F32)
     slot = jnp.sum(earlier, axis=1, keepdims=True)
-    target = own_ref[...].astype(F32) * cap + slot
-    count = teach_ref.shape[0]
-    pick = (iota((tok, count), 1).astype(F32) == target).astype(F32).astype(BF16)
-    teacher_lp = log_probs(mm(pick, teach_ref[...]))
-    student_lp = log_probs(log_ref[...] / own)
+    owner = own_ref[...].astype(F32)
+    for copy in teachers:
+        copy.wait()
+    width = tbuf.shape[1]
+    teacher = jnp.zeros((tok, experts), F32)
+    for j in range(n_seq):
+        pick = (owner == j) & (iota((tok, width), 1).astype(F32) == slot)
+        teacher = teacher + mm(pick.astype(F32).astype(BF16), tbuf[j])
+    teacher_lp = log_probs(teacher)
     prob = jnp.exp(teacher_lp)
+
+    total = log_ref[pl.ds(pl.multiple_of(tile * tok, tok), tok), :]
+    for o, copy in enumerate(logs):
+        copy.wait()
+        total = total + lbuf[o + 1]
+    student_lp = log_probs(total / own)
     kl = jnp.sum(prob * (teacher_lp - student_lp), axis=-1, keepdims=True)
     kl = jnp.sum(kl, axis=0, keepdims=True)
-    g_ref[0:tok, :] = ((jnp.exp(student_lp) - prob) / own).astype(BF16)
+    grad = ((jnp.exp(student_lp) - prob) / own).astype(BF16)
     high, rest = split(kl)
     low = kl - high.astype(F32) - rest.astype(F32)
     line = iota((EXTRA, experts), 0)
-    g_ref[tok : tok + EXTRA, :] = jnp.where(
+    tail = jnp.where(
         line == 0, high.astype(F32), jnp.where(line == 1, rest.astype(F32), jnp.where(line == 2, low, 0.0))
     ).astype(BF16)
-
-
-def router_kernel(regions, sum_ref, g_ref, out_ref):
+    gbuf[tile] = jnp.concatenate([grad, tail], axis=0)
+    copies = [
+        send(gbuf.at[tile], gbuf.at[tile], gsems, o, tile_place(lax.rem(tile + o, regions)))
+        for o in range(1, regions)
+    ]
+    for copy in copies:
+        copy.start()
+    for copy in copies:
+        copy.wait()
+    for r in range(regions):
+        out_ref[r * (tok + EXTRA) : (r + 1) * (tok + EXTRA), :] = gbuf[r]
+
+
+def router_kernel(regions, n_seq, sum_ref, g_ref, out_ref, kl_ref, mine, came, done, asems, bsems):
     tok = sum_ref.shape[0] // regions
     wide = sum_ref.shape[1]
+    part = wide // n_seq
+    me = lax.axis_index("seq")
+    barrier = pltpu.get_barrier_semaphore()
+    for o in range(1, n_seq):
+        signal(barrier, {"seq": lax.rem(me + o, n_seq)})
     total = jnp.zeros((wide, g_ref.shape[1]), F32)
     kl = jnp.zeros((EXTRA, g_ref.shape[1]), F32)
     for r in range(regions):
@@ -198,10 +321,30 @@
         high, low = split(sum_ref[r * tok : (r + 1) * tok, :])
         total = total + mm_tn(jnp.concatenate([high, low], axis=0), jnp.concatenate([g, g], axis=0))
         kl = kl + g_ref[first + tok : first + tok + EXTRA, :].astype(F32)
-    out_ref[0:wide, :] = total
-    out_ref[wide : wide + 8, :] = jnp.broadcast_to(
-        jnp.sum(kl, axis=0, keepdims=True), (8, g_ref.shape[1])
-    )
+    kl = jnp.broadcast_to(jnp.sum(kl, axis=0, keepdims=True), (8, g_ref.shape[1]))
+    for p in range(n_seq):
+        mine[p, 0:part, :] = total[p * part : (p + 1) * part]
+        mine[p, part : part + 8, :] = kl
+    pl.semaphore_wait(barrier, n_seq - 1)
+    copies = []
+    for o in range(1, n_seq):
+        peer = lax.rem(me + o, n_seq)
+        copies.append(send(mine.at[peer], came.at[o], asems, o, {"seq": peer}))
+        copies[-1].start()
+    summed = mine[me]
+    for o, copy in enumerate(copies):
+        copy.wait()
+        summed = summed + came[o + 1]
+    done[me] = summed
+    copies = []
+    for o in range(1, n_seq):
+        copies.append(send(done.at[me], done.at[me], bsems, o, {"seq": lax.rem(me + o, n_seq)}))
+        copies[-1].start()
+    for copy in copies:
+        copy.wait()
+    for p in range(n_seq):
+        out_ref[p * part : (p + 1) * part, :] = done[p, 0:part, :]
+    kl_ref[...] = done[0, part : part + 8, 0:128]
 
 
 def heads_kernel(heads, lens_ref, head_ref, g_ref, w_ref, out_ref):
@@ -223,13 +366,12 @@
         out_ref[:, h, :] = (grad - unit * mean) * inverse
 
 
-def shifted(value, axis, steps):
-    count = lax.axis_size(axis)
-    return lax.ppermute(value, axis, [(source, source + steps) for source in range(count - steps)])
-
-
-def params():
-    return pltpu.CompilerParams(vmem_limit_bytes=LIMIT)
+def params(number=None):
+    if number is None:
+        return pltpu.CompilerParams(vmem_limit_bytes=LIMIT)
+    return pltpu.CompilerParams(
+        vmem_limit_bytes=LIMIT, collective_id=number, has_side_effects=True
+    )
 
 
 def cost(flops, size):
@@ -256,12 +398,13 @@
     cap = teacher_logits.shape[3]
     experts = teacher_logits.shape[4]
     sds = jax.ShapeDtypeStruct
-
-    teacher = lax.all_to_all(
-        teacher_logits.reshape(n_seq, cap, experts), "seq", split_axis=0, concat_axis=0, tiled=True
-    ).reshape(n_seq * cap, experts)
-    lens_all = lax.all_gather(lens, ("head", "tp"), axis=0, tiled=True)
-
+    slots = -(-cap // 16) * 16
+    teacher = teacher_logits.reshape(n_seq, cap, experts)
+    if slots > cap:
+        teacher = jnp.pad(teacher, ((0, 0), (0, slots - cap), (0, 0)))
+
+    tile_sems = pltpu.SemaphoreType.DMA((2, regions))
+    seq_sems = pltpu.SemaphoreType.DMA((2, n_seq))
     step = PAIR * BLOCK
     whole = lambda shape: pl.BlockSpec(shape, lambda i: (0,) * len(shape))
     by_rows = pl.BlockSpec((step, heads, width), lambda i: (i, 0, 0))
@@ -282,12 +425,21 @@
         cost_estimate=cost(30_000_000_000, 20_000_000),
         name="delta",
     )(queries, key_rows, values, log_decay, write_rate)
-    dev_add, dev_map = ends[:, :, :width], ends[:, :, width:]
-
-    state = shifted(dev_add, "seq", 1) if n_seq > 1 else jnp.zeros_like(dev_add)
-    for _ in range(n_seq - 2):
-        moved = jnp.einsum("hij,hjk->hik", dev_map, state, precision=UPPER_LIMIT) + dev_add
-        state = shifted(moved, "seq", 1)
+    lanes = -(-tok // 128) * 128
+    state, lens_all = pl.pallas_call(
+        functools.partial(relay_kernel, heads, n_seq, regions),
+        out_shape=[sds((heads, width, width), F32), sds((regions, lanes), jnp.int32)],
+        scratch_shapes=[
+            pltpu.VMEM((heads, width, width), F32),
+            pltpu.VMEM((heads, width, width), F32),
+            pltpu.VMEM((regions, 8, lanes), jnp.int32),
+            pltpu.SemaphoreType.DMA((2, heads)),
+            tile_sems,
+        ],
+        compiler_params=params(1),
+        name="relay",
+    )(ends, jnp.broadcast_to(jnp.pad(lens, ((0, 0), (0, lanes - tok))), (8, lanes)))
+    lens_all = lens_all[:, :tok]
 
     by_region = pl.BlockSpec((heads, region, width), lambda i: (0, i, 0))
     head_out, sums, partial = pl.pallas_call(
@@ -315,23 +467,30 @@
         name="pool",
     )(lens_all, local, reach, state, router_weight)
 
-    summed = lax.psum_scatter(partial, ("head", "tp"), scatter_dimension=0, tiled=True)
-    grads = pl.pallas_call(
-        functools.partial(loss_kernel, cap),
-        out_shape=sds((tok + EXTRA, experts), BF16),
-        compiler_params=params(),
+    gathered = pl.pallas_call(
+        functools.partial(loss_kernel, cap, n_seq, regions),
+        out_shape=sds((regions * (tok + EXTRA), experts), BF16),
+        scratch_shapes=[
+            pltpu.VMEM((n_seq, slots, experts), BF16),
+            pltpu.VMEM((regions, tok, experts), F32),
+            pltpu.VMEM((regions, tok + EXTRA, experts), BF16),
+            seq_sems,
+            tile_sems,
+            tile_sems,
+        ],
+        compiler_params=params(2),
         name="loss",
-    )(lens, span_owner.reshape(tok, 1), span_owner.reshape(1, tok), teacher, summed)
-    gathered = lax.all_gather(grads, ("head", "tp"), axis=0, tiled=True)
-
-    router = pl.pallas_call(
-        functools.partial(router_kernel, regions),
-        out_shape=sds((heads * width + 8, experts), F32),
-        compiler_params=params(),
+    )(lens, span_owner.reshape(tok, 1), span_owner.reshape(1, tok), teacher, partial)
+
+    router, kl = pl.pallas_call(
+        functools.partial(router_kernel, regions, n_seq),
+        out_shape=[sds((heads * width, experts), F32), sds((8, 128), F32)],
+        scratch_shapes=[pltpu.VMEM((n_seq, heads * width // n_seq + 8, experts), F32)] * 3
+        + [seq_sems, seq_sems],
+        compiler_params=params(3),
         cost_estimate=cost(300_000_000, 2_000_000),
         name="router",
     )(sums, gathered)
-    router = lax.psum(router, "seq")
     grad_heads = pl.pallas_call(
         functools.partial(heads_kernel, heads),
         grid=(regions,),
@@ -347,8 +506,8 @@
         cost_estimate=cost(3_000_000_000, 12_000_000),
         name="heads",
     )(lens_all, head_out, gathered, router_weight)
-    grad_router = router[: heads * width].reshape(heads, width, experts)
-    mean_kl = router[heads * width, :1] / (tok * n_seq * regions)
+    grad_router = router.reshape(heads, width, experts)
+    mean_kl = kl[0, :1] / (tok * n_seq * regions)
     return (grad_router, grad_heads, mean_kl)
 
 

time: 191 us -> 144 us (0.75)
  waiting for transfers between devices: 58.2 us -> 0 us
  Pallas kernels: 74.9 us -> 132 us
  starting transfers between devices: 18.4 us -> 0 us
  between operations: 15.9 us -> 2.5 us
  blocking collectives: 10.9 us -> 0 us
  local copies, waits for them, and re-layouts: 11 us -> 8.32 us
    pallas_call x2 -> x3, Pallas kernels: 1.96 us -> 58.8 us  [the longest x1 27 us: shards(): pl.pallas_call(functools.partial(router_kernel, regions, n_seq), out_shap...]
    psum x1 -> x0, waiting for transfers between devices: 29.9 us -> none  [shards(): router = lax.psum(router, 'seq')]
    ppermute x3 -> x0, starting transfers between devices: 13.7 us -> none  [shifted(): lax.ppermute(value, axis, [(source, source + steps) for source in range(c...]
    all_gather x2 -> x0, blocking collectives: 10.9 us -> none  [the longest x1 5.88 us: shards(): gathered = lax.all_gather(grads, ('head', 'tp'), axis=0, tiled=True)]
    ppermute x3 -> x0, waiting for transfers between devices: 10.2 us -> none  [shifted(): lax.ppermute(value, axis, [(source, source + steps) for source in range(c...]
    reduce_scatter x1 -> x0, waiting for transfers between devices: 9.54 us -> none  [shards(): lax.psum_scatter(partial, ('head', 'tp'), scatter_dimension=0, tiled=True)]
    all_to_all x1 -> x0, waiting for transfers between devices: 8.51 us -> none  [shards(): lax.all_to_all(teacher_logits.reshape(n_seq, cap, experts), 'seq', split_...]
    all_to_all x1 -> x0, starting transfers between devices: 4.58 us -> none  [shards(): lax.all_to_all(teacher_logits.reshape(n_seq, cap, experts), 'seq', split_...]
  transfers between devices with their start and end apart: 6 -> 0, of which waited for: 5 -> 0; matrix products, arithmetic and copies ran while one was open for 0% -> 0% of each run, Pallas kernels for 4% -> 0%
where the time goes in v2:
time: 144 us; the launch traced here: 142 us
  Pallas kernels  132 us (92%)
  local copies, waits for them, and re-layouts  8.32 us (6%)
  between operations  2.5 us (2%)
    pallas_call x1, Pallas kernels, shards(): pl.pallas_call(functools.partial(delta_kernel, heads), grid=(rows // step...  54.4 us
    pallas_call x1, Pallas kernels, shards(): pl.pallas_call(functools.partial(router_kernel, regions, n_seq), out_shap...  27 us
    pallas_call x1, Pallas kernels, shards(): pl.pallas_call(functools.partial(loss_kernel, cap, n_seq, regions), out_s...  21 us
    pallas_call x1, Pallas kernels, shards(): pl.pallas_call(functools.partial(pool_kernel, heads), grid=(regions,), in...  11.7 us
    pallas_call x1, Pallas kernels, shards(): pl.pallas_call(functools.partial(relay_kernel, heads, n_seq, regions), ou...  10.8 us
    unnamed x19, local copies, waits for them, and re-layouts  7.69 us
    pallas_call x1, Pallas kernels, shards(): pl.pallas_call(functools.partial(heads_kernel, heads), grid=(regions,), i...  6.7 us

profile of v2, /device:TPU:0, one launch (start us, length us, event | category | flops | bytes accessed | tf_op | source)
XLA Modules:
  0.0 142.4 jit_solution(10456857691007399620)
XLA Ops:
  0.6 0.0 copy-start.2
  0.6 0.0 copy-start.3
  0.7 1.6 %copy-done.3 = bf16[2048,4,128]{2,1,0:T(4,128)(2,1)S(1)} copy-done((bf16[2048,4,128]{2,1,0:T(4,128)(2,1)S(1)}, bf16[2048,4,128]{2,1,0:T(4,128)(2,1)}, u32[]{:S(2)}) %copy-start.3) | copy-done | bytes 2097176
  2.2 0.0 copy-start.4
  2.2 1.6 %copy-done.4 = bf16[2048,4,128]{2,1,0:T(4,128)(2,1)S(1)} copy-done((bf16[2048,4,128]{2,1,0:T(4,128)(2,1)S(1)}, bf16[2048,4,128]{2,1,0:T(4,128)(2,1)}, u32[]{:S(2)}) %copy-start.4) | copy-done | bytes 2097176
  3.8 0.0 copy-start.6
  3.8 0.8 copy-done.6
  4.6 0.0 copy-start.7
  4.6 0.8 copy-done.7
  5.3 0.0 copy-start.5
  5.4 54.4 %delta.1 = (f32[4,2048,128]{2,1,0:T(8,128)}, f32[4,2048,128]{2,1,0:T(8,128)}, f32[4,128,256]{2,1,0:T(8,128)S(1)}) custom-call(bf16[2048,4,128]{2,1,0:T(4,128)(2,1)S(1)} %copy-done.3, bf16[2048,4,128]{2,1,0:T(4,128)(2,1)S(1)} %copy-done.4, bf16[2048,4,128]{2,1,0:T(4,128)(2,1)} %v_ref.1, f32[4,2048]{1,0:T(4,128)S(1)} %copy-done.6, f32[4,2048]{1,0:T(4,128)S(1)} %copy-done.7), custom_call_target="tpu_custom_call" | custom-call | flops 30000001024 | bytes 20000000 | tf_op jit(solution)/shard_map/delta/pallas_call | solution.py:413
  59.8 0.0 copy-done.2
  59.8 10.8 %relay.1 = (f32[4,128,128]{2,1,0:T(8,128)S(1)}, s32[4,128]{1,0:T(4,128)S(1)}) custom-call(f32[4,128,256]{2,1,0:T(8,128)S(1)} %get-tuple-element.13.ends_ref, s32[8,128]{1,0:T(8,128)S(1)} %broadcast_in_dim.8.lens_ref), custom_call_target="tpu_custom_call" | custom-call | tf_op jit(solution)/shard_map/relay/pallas_call | solution.py:429
  70.6 0.0 copy-done.5
  70.6 0.0 copy-start.1
  70.6 0.0 copy-start
  70.6 11.7 %pool.1 = (f32[4,2048,128]{2,1,0:T(8,128)}, f32[512,512]{1,0:T(8,128)S(1)}, f32[512,256]{1,0:T(8,128)S(1)}) custom-call(s32[4,128]{1,0:T(4,128)S(1)} %get-tuple-element.14.lens_ref, f32[4,2048,128]{2,1,0:T(8,128)} %get-tuple-element.15.loc_ref, f32[4,2048,128]{2,1,0:T(8,128)} %get-tuple-element.16.reach_ref, f32[4,128,128]{2,1,0:T(8,128)S(1)} %get-tuple-element.17.s_ref, ...), custom_call_target="tpu_custom_call" | custom-call | flops 3000000000 | bytes 16000000 | tf_op jit(solution)/shard_map/pool/pallas_call | solution.py:445
  82.3 0.0 copy-done.1
  82.3 0.1 copy.12.own_ref
  82.4 0.0 copy-done
  82.4 21.0 %loss.1.g_ref = bf16[576,256]{1,0:T(8,128)(2,1)S(1)} custom-call(s32[1,128]{1,0:T(1,128)S(1)} %bitcast.12, s32[128,1]{1,0:T(8,128)S(1)} %copy.12.own_ref, s32[1,128]{1,0:T(1,128)S(1)} %bitcast.10, bf16[4,128,256]{2,1,0:T(8,128)(2,1)S(1)} %bitcast.8, f32[512,256]{1,0:T(8,128)S(1)} %get-tuple-element.19.log_ref), custom_call_target="tpu_custom_call" | custom-call | tf_op jit(solution)/shard_map/loss/pallas_call | solution.py:470
  103.5 0.0 copy-start.8
  103.5 2.2 %copy-done.8 = f32[4,2048,128]{2,1,0:T(8,128)S(1)} copy-done((f32[4,2048,128]{2,1,0:T(8,128)S(1)}, f32[4,2048,128]{2,1,0:T(8,128)}, u32[]{:S(2)}) %copy-start.8) | copy-done | bytes 4194328
  105.7 6.7 %heads.1 = f32[2048,4,128]{2,1,0:T(4,128)} custom-call(s32[4,128]{1,0:T(4,128)S(1)} %get-tuple-element.14.lens_ref, f32[4,2048,128]{2,1,0:T(8,128)S(1)} %copy-done.8, bf16[576,256]{1,0:T(8,128)(2,1)S(1)} %loss.1.g_ref, bf16[4,128,256]{2,1,0:T(8,128)(2,1)S(1)} %copy-done.5), custom_call_target="tpu_custom_call" | custom-call | flops 3000000000 | bytes 12000000 | tf_op jit(solution)/shard_map/heads/pallas_call | solution.py:494
  112.4 27.0 %router.1 = (f32[512,256]{1,0:T(8,128)S(1)}, f32[8,128]{1,0:T(8,128)S(1)}) custom-call(f32[512,512]{1,0:T(8,128)S(1)} %get-tuple-element.18.sum_ref, bf16[576,256]{1,0:T(8,128)(2,1)S(1)} %loss.1.g_ref), custom_call_target="tpu_custom_call" | custom-call | flops 300000000 | bytes 2000000 | tf_op jit(solution)/shard_map/router/pallas_call | solution.py:485
  139.3 0.5 slice.3
  140.5 0.8 copy.14
  (1 shorter events, 0.0 us)
Async XLA Ops:
  0.6 59.2 %copy-start.2 = (s32[1,1,128]{2,1,0:T(1,128)S(1)}, s32[1,1,128]{2,1,0:T(1,128)}, u32[]{:S(2)}) copy-start(s32[1,1,128]{2,1,0:T(1,128)} %param.16) | copy-start | bytes 1540
  0.6 1.6 %copy-start.3 = (bf16[2048,4,128]{2,1,0:T(4,128)(2,1)S(1)}, bf16[2048,4,128]{2,1,0:T(4,128)(2,1)}, u32[]{:S(2)}) copy-start(bf16[2048,4,128]{2,1,0:T(4,128)(2,1)} %q_ref.1) | copy-start | bytes 6291460
  2.2 1.6 %copy-start.4 = (bf16[2048,4,128]{2,1,0:T(4,128)(2,1)S(1)}, bf16[2048,4,128]{2,1,0:T(4,128)(2,1)}, u32[]{:S(2)}) copy-start(bf16[2048,4,128]{2,1,0:T(4,128)(2,1)} %k_ref.1) | copy-start | bytes 6291460
  3.8 0.8 copy-start.6
  4.6 0.8 copy-start.7
  5.3 65.2 %copy-start.5 = (bf16[4,128,256]{2,1,0:T(8,128)(2,1)S(1)}, bf16[4,128,256]{2,1,0:T(8,128)(2,1)}, u32[]{:S(2)}) copy-start(bf16[4,128,256]{2,1,0:T(8,128)(2,1)} %w_ref.3) | copy-start | bytes 786436
  70.6 11.8 %copy-start.1 = (s32[1,1,128,1]{2,3,1,0:T(1,128)S(1)}, s32[1,1,128,1]{2,3,1,0:T(1,128)}, u32[]{:S(2)}) copy-start(s32[1,1,128,1]{2,3,1,0:T(1,128)} %param.17) | copy-start | bytes 1540
  70.6 11.9 %copy-start = (bf16[1,1,4,128,256]{4,3,2,1,0:T(8,128)(2,1)S(1)}, bf16[1,1,4,128,256]{4,3,2,1,0:T(8,128)(2,1)}, u32[]{:S(2)}) copy-start(bf16[1,1,4,128,256]{4,3,2,1,0:T(8,128)(2,1)} %param.15) | copy-start | bytes 786436
  103.5 2.2 %copy-start.8 = (f32[4,2048,128]{2,1,0:T(8,128)S(1)}, f32[4,2048,128]{2,1,0:T(8,128)}, u32[]{:S(2)}) copy-start(f32[4,2048,128]{2,1,0:T(8,128)} %get-tuple-element.21.head_ref) | copy-start | bytes 12582916
